TPU v7x, 512 devices: a whole 4x8x8 slice. The times are simulated.
512 devices in a mesh: row: 32 (over z, x), col: 16 (over y, core).
Axes of the slice: x: 4, y: 8, z: 8, core: 2. Of those that a mesh axis runs over, the one named last changes fastest.
Arguments:
- vectors: bfloat16 [64, 262144], P(None, ('row', 'col')), may hold values from -6 to 6
- tiles: bfloat16 [12288, 256, 256], P(('row', 'col')), may hold values from -0.125 to 0.125
- tile_row: int32 [12288], P(('row', 'col')), may hold values from 0 to 31
- tile_col: int32 [12288], P(('row', 'col')), may hold values from 0 to 63
- tile_count: int32 [512], P(('row', 'col')), may hold values from 1 to 24, 7680 in all
- lower: float32 [1], replicated, may hold values from -1.5 to -0.5
- upper: float32 [1], replicated, may hold values from 0.5 to 1.5
Outputs:
- filtered: bfloat16 [64, 262144], P(None, ('row', 'col'))
Inputs may be any that keep to these rules, and one draw needn't show every extreme that they name: `tile_row`: block rows of a slot inside its device's row panel. `tile_col`: block columns of a slot inside its device's column panel. `tile_count`: slots past a device's count are ignored; some device uses all 24 slots.
All inputs are finite; a program needn't handle non-finite values.
Results may differ from a plain program's by a relative error of at most 0.023.
Values may be sent and summed in bfloat16 or wider, within the bound.
No kernel may reach another device: no remote copies, remote signals or barrier semaphores. Data moves between devices by JAX's collectives and lax.ppermute only.
A program may use at most 64 MiB of HBM per device.

v0:
```python
import jax
import jax.numpy as jnp
from jax import lax
from jax.sharding import PartitionSpec as P

TB = 256
DEGREE = 2


def from_root(value, axis, source):
    kept = jnp.where(lax.axis_index(axis) == source, value, 0).astype(value.dtype)
    return lax.psum(kept, axis)


def row_panel(piece):
    return lax.all_gather(piece, "col", axis=1, tiled=True)


def column_panel(panel):
    ratio = lax.axis_size("row") // lax.axis_size("col")
    pieces = []
    for part_index in range(ratio):
        root = ratio * lax.axis_index("col") + part_index
        pieces.append(from_root(panel, "row", root))
    return jnp.concatenate(pieces, axis=1)


def local_product(columns, tiles, tile_row, tile_col, tile_count, panel_width):
    count_vec = columns.shape[0]
    blocks = columns.reshape(count_vec, -1, TB)
    picked = jnp.take(blocks, tile_col, axis=1)
    prod = jnp.einsum("vtk,tjk->tvj", picked, tiles, preferred_element_type=jnp.float32)
    slots = tiles.shape[0]
    block_rows = panel_width // TB
    live = (jnp.arange(slots, dtype=jnp.int32) < tile_count[0]).astype(jnp.float32)
    onehot = (tile_row[None, :] == jnp.arange(block_rows, dtype=jnp.int32)[:, None]).astype(
        jnp.float32
    ) * live[None, :]
    part = jnp.einsum("bt,tvj->vbj", onehot, prod, precision=lax.Precision.HIGHEST)
    return part.reshape(count_vec, panel_width)


def recurrence(sums, current, previous, center, half, step):
    shifted = (sums - center * current.astype(jnp.float32)) / half
    if step == 0:
        return shifted.astype(jnp.bfloat16)
    return (2.0 * shifted - previous.astype(jnp.float32)).astype(jnp.bfloat16)


def on_device(vectors, tiles, tile_row, tile_col, tile_count, lower, upper):
    center = (upper[0] + lower[0]) / 2.0
    half = (upper[0] - lower[0]) / 2.0
    shard_width = vectors.shape[1]
    panel_width = shard_width * lax.axis_size("col")
    current = vectors
    previous = vectors
    for step in range(DEGREE):
        columns, mapped = (column_panel(row_panel(current)), tile_col)
        partial_value = local_product(columns, tiles, tile_row, mapped, tile_count, panel_width)
        sums = lax.psum_scatter(
            partial_value.astype(jnp.bfloat16), "col", scatter_dimension=1, tiled=True
        ).astype(jnp.float32)
        following = recurrence(sums, current, previous, center, half, step)
        previous, current = (current, following)
    return current


def solution(mesh):
    return jax.shard_map(
        on_device,
        mesh=mesh,
        in_specs=(
            P(None, ("row", "col")),
            P(("row", "col"), None, None),
            P(("row", "col")),
            P(("row", "col")),
            P(("row", "col")),
            P(),
            P(),
        ),
        out_specs=P(None, ("row", "col")),
        check_vma=False,
    )
```

profile of v0, /device:TPU:1, one launch (start us, length us, event | category | flops | bytes accessed | tf_op | source)
XLA Modules:
  0.0 580.7 jit_solution(13611889829618445478)
XLA Ops:
  6.5 0.0 copy-start
  6.5 0.0 all-gather.3.cloned.1.call-start
  6.5 0.7 all-gather.3.cloned.1.call-update
  7.3 0.0 all-reduce.7.cloned.1.call-start
  7.3 0.0 copy-start.4
  7.3 48.9 %all-gather.3.cloned.1.call-done = bf16[64,8192]{1,0:T(8,128)(2,1)} async-done(((bf16[64,512]{1,0:T(8,128)(2,1)}), bf16[64,8192]{1,0:T(8,128)(2,1)}) %all-gather.3.cloned.1.call-update) | async-done | bytes 1048592 | tf_op jit(solution)/shard_map/all_gather | solution.py:16
  56.3 2.7 broadcast_select_fusion.3
  59.0 0.0 all-reduce.7.cloned.1.call-update
  59.0 0.0 reduce-scatter.3.cloned.1.call-start
  59.7 0.0 copy-done.4
  59.8 160.8 %all-reduce.7.cloned.1.call-done = (bf16[64,8192]{1,0:T(8,128)(2,1)}, bf16[64,8192]{1,0:T(8,128)(2,1)}) async-done(((bf16[64,8192]{1,0:T(8,128)(2,1)}, bf16[64,8192]{1,0:T(8,128)(2,1)}), (bf16[64,8192]{1,0:T(8,128)(2,1)}, bf16[64,8192]{1,0:T(8,128)(2,1)})) %all-reduce.7.cloned.1.call-update) | async-done | bytes 2097168 | tf_op jit(solution)/shard_map/psum | solution.py:12
  220.6 1.7 pad_maximum_fusion
  222.3 1.6 copy.27
  223.9 3.1 gather_fusion
  227.0 0.0 copy-done
  227.0 0.0 copy-start.3
  227.0 2.2 fusion.12
  229.2 0.0 copy-done.3
  229.2 2.9 fusion.4
  232.2 0.0 copy-start.1
  232.2 1.6 copy.14
  233.8 0.0 reduce-scatter.3.cloned.1.call-update
  233.8 0.0 all-gather.5.cloned.1.call-start
  235.2 57.3 %reduce-scatter.3.cloned.1.call-done = bf16[64,512]{1,0:T(8,128)(2,1)} async-done(((bf16[64,8192]{1,0:T(8,128)(2,1)}), bf16[64,512]{1,0:T(8,128)(2,1)}) %reduce-scatter.3.cloned.1.call-update) | async-done | bytes 65552 | tf_op jit(solution)/shard_map/reduce_scatter | solution.py:60
  292.5 0.0 copy-done.1
  292.5 1.5 fusion.22
  294.0 0.0 all-gather.5.cloned.1.call-update
  294.0 0.0 all-reduce.5.cloned.1.call-start
  294.0 42.3 %all-gather.5.cloned.1.call-done = bf16[64,8192]{1,0:T(8,128)(2,1)} async-done(((bf16[64,512]{1,0:T(8,128)(2,1)}), bf16[64,8192]{1,0:T(8,128)(2,1)}) %all-gather.5.cloned.1.call-update) | async-done | bytes 1048592 | tf_op jit(solution)/shard_map/all_gather | solution.py:16
  336.3 2.7 broadcast_select_fusion.2
  339.0 0.0 all-reduce.5.cloned.1.call-update
  339.0 0.0 reduce-scatter.5.cloned.1.call-start
  339.1 161.4 %all-reduce.5.cloned.1.call-done = (bf16[64,8192]{1,0:T(8,128)(2,1)}, bf16[64,8192]{1,0:T(8,128)(2,1)}) async-done(((bf16[64,8192]{1,0:T(8,128)(2,1)}, bf16[64,8192]{1,0:T(8,128)(2,1)}), (bf16[64,8192]{1,0:T(8,128)(2,1)}, bf16[64,8192]{1,0:T(8,128)(2,1)})) %all-reduce.5.cloned.1.call-update) | async-done | bytes 2097168 | tf_op jit(solution)/shard_map/psum | solution.py:12
  500.5 1.7 pad_maximum_fusion.1
  502.2 1.6 copy.26
  503.8 3.1 gather_fusion.1
  506.9 2.2 fusion.10
  509.1 2.9 fusion.7
  512.1 0.0 copy-start.2
  512.1 1.6 copy.15
  513.7 0.0 reduce-scatter.5.cloned.1.call-update
  513.7 58.6 %reduce-scatter.5.cloned.1.call-done = bf16[64,512]{1,0:T(8,128)(2,1)} async-done(((bf16[64,8192]{1,0:T(8,128)(2,1)}), bf16[64,512]{1,0:T(8,128)(2,1)}) %reduce-scatter.5.cloned.1.call-update) | async-done | bytes 65552 | tf_op jit(solution)/shard_map/reduce_scatter | solution.py:60
  572.4 0.0 copy-done.2
  572.4 1.5 fusion.23
  (4 shorter events, 0.0 us)
Async XLA Ops:
  6.5 220.5 %copy-start = (bf16[24,256,256]{2,1,0:T(8,128)(2,1)S(1)}, bf16[24,256,256]{2,1,0:T(8,128)(2,1)}, u32[]{:S(2)}) copy-start(bf16[24,256,256]{2,1,0:T(8,128)(2,1)} %param.10) | copy-start | bytes 9437188
  6.5 49.7 %all-gather.3.cloned.1.call-start = ((), (), s32[]{:S(2)}) async-start(), calls=%async_computation.2 | async-start | bytes 1114112 | tf_op jit(solution)/shard_map/all_gather | solution.py:16
  7.3 213.3 %all-reduce.7.cloned.1.call-start = ((), (), s32[]{:S(2)}) async-start(), calls=%async_computation.7 | async-start | bytes 4194304 | tf_op jit(solution)/shard_map/psum | solution.py:12
  7.3 52.4 %copy-start.4 = (s32[24]{0:T(128)S(1)}, s32[24]{0:T(128)}, u32[]{:S(2)}) copy-start(s32[24]{0:T(128)} %param.12) | copy-start | bytes 292
  59.0 233.5 %reduce-scatter.3.cloned.1.call-start = ((), (), s32[]{:S(2)}) async-start(), calls=%async_computation.3 | async-start | bytes 1114112 | tf_op jit(solution)/shard_map/reduce_scatter | solution.py:60
  227.0 2.2 copy-start.3
  232.2 60.3 %copy-start.1 = (bf16[64,512]{1,0:T(8,128)(2,1)S(1)}, bf16[64,512]{1,0:T(8,128)(2,1)}, u32[]{:S(2)}) copy-start(bf16[64,512]{1,0:T(8,128)(2,1)} %param.9) | copy-start | bytes 196612
  233.8 102.5 %all-gather.5.cloned.1.call-start = ((), (), s32[]{:S(2)}) async-start(), calls=%async_computation.4 | async-start | bytes 1114112 | tf_op jit(solution)/shard_map/all_gather | solution.py:16
  294.0 206.5 %all-reduce.5.cloned.1.call-start = ((), (), s32[]{:S(2)}) async-start(), calls=%async_computation.6 | async-start | bytes 4194304 | tf_op jit(solution)/shard_map/psum | solution.py:12
  339.0 233.3 %reduce-scatter.5.cloned.1.call-start = ((), (), s32[]{:S(2)}) async-start(), calls=%async_computation.5 | async-start | bytes 1114112 | tf_op jit(solution)/shard_map/reduce_scatter | solution.py:60
  512.1 60.3 %copy-start.2 = (bf16[64,512]{1,0:T(8,128)(2,1)S(1)}, bf16[64,512]{1,0:T(8,128)(2,1)}, u32[]{:S(2)}) copy-start(bf16[64,512]{1,0:T(8,128)(2,1)} %reduce-scatter.3.cloned.1.call-done) | copy-start | bytes 196612
Sparse Core Ops, SparseCore 0:
  9.5 46.7 all-gather.2
  59.9 160.6 all-reduce.6
  234.0 58.4 reduce-scatter.2
  294.5 41.7 all-gather.4
  339.8 160.6 all-reduce.4
  513.8 58.4 reduce-scatter.4
where the time goes:
time: 582 us; the launch traced here: 581 us
  waiting for transfers between devices  530 us (91%)
  between operations  15.5 us (3%)
  local copies, waits for them, and re-layouts  12.7 us (2%)
  other arithmetic  11.8 us (2%)
  matrix products  10.3 us (2%)
    psum x2, waiting for transfers between devices, from_root(): return lax.psum(kept, axis)  322 us
    reduce_scatter x2, waiting for transfers between devices, on_device(): lax.psum_scatter(partial_value.astype(jnp.bfloat16), 'col', scatter_dimen...  116 us
    all_gather x2, waiting for transfers between devices, row_panel(): return lax.all_gather(piece, 'col', axis=1, tiled=True)  91.2 us
  transfers between devices with their start and end apart: 6, of which 6 were waited for; matrix products, arithmetic and copies ran while one was open for 0% of the time, Pallas kernels for 0%

commit v1 on v0

v1 whole, which is shorter than its diff:
```python
import functools

import jax
import jax.numpy as jnp
from jax import lax
from jax.experimental import pallas as pl
from jax.experimental.pallas import tpu as pltpu
from jax.sharding import PartitionSpec as P

NZ, NX, NY, NC = 8, 4, 8, 2
TB = 256
NV = 64
SLOTS = 24
BR = 32
DEGREE = 2
PIECE = 2 * TB
AXES = ("row", "col")

PLACES = [(z, x, y, c) for z in range(NZ) for x in range(NX) for y in range(NY) for c in range(NC)]


def number(z, x, y, c):
    return (((z % NZ) * NX + x % NX) * NY + y % NY) * NC + c % NC


def permute(value, move):
    return lax.ppermute(value, AXES, [(number(*p), number(*move(*p))) for p in PLACES])


def grouped(key):
    groups = {}
    for place in PLACES:
        groups.setdefault(key(*place), []).append(number(*place))
    return [sorted(group) for group in groups.values()]


def exchange(value, groups):
    return lax.all_to_all(value, AXES, 0, 0, axis_index_groups=groups, tiled=True)


def class_of(z, x, c):
    return (z + 2 * x) % 4 if c == 0 else (x + 2 * z) % 4


CLASSES = grouped(lambda z, x, y, c: (y, c, class_of(z, x, c)))
LINES = grouped(lambda z, x, y, c: (z, x, c))


def to_column_plane(z, x, y, c):
    return (y, (x % 2) * 2 + c, z, x // 2)


def along(sign):
    return lambda z, x, y, c: (z + sign, x, y, c) if c == 0 else (z, x + sign, y, c)


def across(sign):
    return lambda z, x, y, c: (z, x + sign, y, c) if c == 0 else (z + sign, x, y, c)


def other_core(z, x, y, c):
    return (z, x, y, 1 - c)


def column_panel(piece):
    mine = permute(piece, to_column_plane)
    bundle = exchange(jnp.broadcast_to(mine[None], (8,) + mine.shape), CLASSES)
    below = permute(bundle, along(1))
    above = permute(bundle, along(-1))
    first = permute(bundle[:4], across(1))
    second = permute(bundle[4:], across(-1))
    return bundle, below, above, first, second


def block_places(tile_col, z, x, c):
    from_z = (tile_col % 32) // 4
    from_x = (tile_col // 32) * 2 + (tile_col // 2) % 2
    theirs = jnp.where(c == 0, from_z + 2 * from_x, from_x + 2 * from_z)
    own = jnp.where(c == 0, z + 2 * x, x + 2 * z)
    member = jnp.where(c == 0, (from_z // 2) * 2 + from_x // 2, from_z)
    apart = (theirs - own) % 4
    start = jnp.where(apart == 0, 0, jnp.where(apart == 3, 8, jnp.where(apart == 1, 16, 24)))
    return (start + member) * 2 + tile_col % 2


def product_kernel(
    place_ref, row_ref, core_ref, b0, b1, b2, b3, b4, tiles_hbm,
    keep_ref, give_ref, panel, tiles, total, panel_sems, tile_sems,
):
    chunk = SLOTS // 4
    loads = []
    for index, (source, start, size) in enumerate(
        ((b0, 0, 8), (b1, 8, 8), (b2, 16, 8), (b3, 24, 4), (b4, 28, 4))
    ):
        loads.append(
            pltpu.make_async_copy(source, panel.at[pl.ds(start, size)], panel_sems.at[index])
        )
    tile_loads = []
    for index in range(4):
        part = pl.ds(index * chunk, chunk)
        tile_loads.append(
            pltpu.make_async_copy(tiles_hbm.at[part], tiles.at[part], tile_sems.at[index])
        )
    for load in loads + tile_loads:
        load.start()
    total[...] = jnp.zeros_like(total)
    for load in loads:
        load.wait()
    for index in range(4):
        tile_loads[index].wait()
        slots = range(index * chunk, (index + 1) * chunk)
        products = []
        for slot in slots:
            place = place_ref[slot]
            half = pl.multiple_of((place % 2) * TB, TB)
            block = panel[place // 2, :, pl.ds(half, TB)]
            products.append(
                lax.dot_general(
                    block, tiles[slot], (((1,), (1,)), ((), ())),
                    preferred_element_type=jnp.float32,
                )
            )
        for slot, product in zip(slots, products):
            row = row_ref[slot]
            total[row] = total[row] + product
    core = core_ref[0]
    for line in range(NY):
        for half in range(2):
            columns = slice(half * TB, (half + 1) * TB)
            keep_ref[line, :, columns] = total[4 * line + 2 * core + half].astype(jnp.bfloat16)
            give_ref[line, :, columns] = total[4 * line + 2 * (1 - core) + half].astype(jnp.bfloat16)


def local_product(parts, tiles, places, rows, core):
    half_panel = jax.ShapeDtypeStruct((NY, NV, PIECE), jnp.bfloat16)
    return pl.pallas_call(
        product_kernel,
        out_shape=(half_panel, half_panel),
        in_specs=[pl.BlockSpec(memory_space=pltpu.SMEM)] * 3
        + [pl.BlockSpec(memory_space=pl.ANY)] * 6,
        out_specs=(pl.BlockSpec(memory_space=pltpu.VMEM),) * 2,
        scratch_shapes=[
            pltpu.VMEM((32, NV, PIECE), jnp.bfloat16),
            pltpu.VMEM((SLOTS, TB, TB), jnp.bfloat16),
            pltpu.VMEM((BR + 1, NV, TB), jnp.float32),
            pltpu.SemaphoreType.DMA((5,)),
            pltpu.SemaphoreType.DMA((4,)),
        ],
        compiler_params=pltpu.CompilerParams(vmem_limit_bytes=24 * 1024 * 1024),
        cost_estimate=pl.CostEstimate(
            flops=2 * SLOTS * NV * TB * TB, bytes_accessed=8 * 1024 * 1024, transcendentals=0
        ),
        name="block_products",
    )(places, rows, core, *parts, tiles)


def recurrence(sums, current, previous, center, half, step):
    shifted = (sums - center * current.astype(jnp.float32)) / half
    if step == 0:
        return shifted.astype(jnp.bfloat16)
    return (2.0 * shifted - previous.astype(jnp.float32)).astype(jnp.bfloat16)


def on_device(vectors, tiles, tile_row, tile_col, tile_count, lower, upper):
    center = (upper[0] + lower[0]) / 2.0
    half = (upper[0] - lower[0]) / 2.0
    row, col = lax.axis_index("row"), lax.axis_index("col")
    z, x, core = row // NX, row % NX, col % NC
    places = block_places(tile_col, z, x, core)
    used = jnp.arange(SLOTS, dtype=jnp.int32) < tile_count[0]
    rows = jnp.where(used, tile_row, BR)
    core_ref = core.astype(jnp.int32)[None]
    current = previous = vectors
    for step in range(DEGREE):
        parts = column_panel(current)
        keep, give = local_product(parts, tiles, places, rows, core_ref)
        taken = permute(give, other_core)
        pair = (keep.astype(jnp.float32) + taken.astype(jnp.float32)).astype(jnp.bfloat16)
        sums = jnp.sum(exchange(pair, LINES).astype(jnp.float32), axis=0)
        following = recurrence(sums, current, previous, center, half, step)
        previous, current = (current, following)
    return current


def solution(mesh):
    return jax.shard_map(
        on_device,
        mesh=mesh,
        in_specs=(
            P(None, AXES),
            P(AXES, None, None),
            P(AXES),
            P(AXES),
            P(AXES),
            P(),
            P(),
        ),
        out_specs=P(None, AXES),
        check_vma=False,
    )
```

time: 582 us -> 183 us (0.31)
  waiting for transfers between devices: 530 us -> 42.1 us
  blocking collectives: 0 us -> 85.4 us
  starting transfers between devices: 0.21 us -> 40.9 us
  between operations: 15.5 us -> 2.17 us
  local copies, waits for them, and re-layouts: 12.7 us -> 2.04 us
  matrix products: 10.3 us -> 0 us
  other arithmetic: 11.8 us -> 3.7 us
    psum x2 -> x0, waiting for transfers between devices: 322 us -> none  [from_root(): return lax.psum(kept, axis)]
    reduce_scatter x2 -> x0, waiting for transfers between devices: 116 us -> none  [on_device(): lax.psum_scatter(partial_value.astype(jnp.bfloat16), 'col', scatter_dimen...]
    all_gather x2 -> x0, waiting for transfers between devices: 91.2 us -> none  [row_panel(): return lax.all_gather(piece, 'col', axis=1, tiled=True)]
    all_to_all x0 -> x3, blocking collectives: none -> 85.4 us  [exchange(): lax.all_to_all(value, AXES, 0, 0, axis_index_groups=groups, tiled=True)]
    ppermute x0 -> x12, starting transfers between devices: none -> 35.7 us  [permute(): lax.ppermute(value, AXES, [(number(*p), number(*move(*p))) for p in PLACES])]
    ppermute x0 -> x12, waiting for transfers between devices: none -> 25.4 us  [permute(): lax.ppermute(value, AXES, [(number(*p), number(*move(*p))) for p in PLACES])]
    all_to_all x0 -> x1, waiting for transfers between devices: none -> 16.8 us  [exchange(): lax.all_to_all(value, AXES, 0, 0, axis_index_groups=groups, tiled=True)]
    dot_general x4 -> x0, matrix products: 10.3 us -> none  [the longest x2 5.88 us: local_product(): jnp.einsum('bt,tvj->vbj', onehot, prod, precision=lax.Precision.HIGHEST)]
  transfers between devices with their start and end apart: 6 -> 13, of which waited for: 6 -> 9; matrix products, arithmetic and copies ran while one was open for 0% -> 0% of each run, Pallas kernels for 0% -> 0%
where the time goes in v1:
time: 183 us; the launch traced here: 182 us
  blocking collectives  85.4 us (47%)
  waiting for transfers between devices  42.1 us (23%)
  starting transfers between devices  40.9 us (22%)
  Pallas kernels  5.45 us (3%)
  other arithmetic  3.7 us (2%)
  between operations  2.17 us (1%)
  local copies, waits for them, and re-layouts  2.04 us (1%)
    all_to_all x3, blocking collectives, exchange(): lax.all_to_all(value, AXES, 0, 0, axis_index_groups=groups, tiled=True)  85.4 us
    ppermute x12, starting transfers between devices, permute(): lax.ppermute(value, AXES, [(number(*p), number(*move(*p))) for p in PLACES])  35.7 us
    ppermute x12, waiting for transfers between devices, permute(): lax.ppermute(value, AXES, [(number(*p), number(*move(*p))) for p in PLACES])  25.4 us
    all_to_all x1, waiting for transfers between devices, exchange(): lax.all_to_all(value, AXES, 0, 0, axis_index_groups=groups, tiled=True)  16.8 us
    pallas_call x2, Pallas kernels, local_product(): pl.pallas_call(product_kernel, out_shape=(half_panel, half_panel), in_spe...  5.45 us
    all_to_all x1, starting transfers between devices, exchange(): lax.all_to_all(value, AXES, 0, 0, axis_index_groups=groups, tiled=True)  5.26 us
  transfers between devices with their start and end apart: 13, of which 9 were waited for; matrix products, arithmetic and copies ran while one was open for 0% of the time, Pallas kernels for 0%

profile of v1, /device:TPU:1, one launch (start us, length us, event | category | flops | bytes accessed | tf_op | source)
XLA Modules:
  0.0 181.8 jit_solution(14863863453074296114)
XLA Ops:
  0.0 4.5 %collective-permute-start = (bf16[64,512]{1,0:T(8,128)(2,1)}, bf16[64,512]{1,0:T(8,128)(2,1)S(1)}, u32[]{:S(2)}, u32[]{:S(2)}) collective-permute-start(bf16[64,512]{1,0:T(8,128)(2,1)} %param.7), channel_id=1, source_target_pairs={{0,0},{1,16},{2,64},{3,80},{4,128},{5,144},{6,192},{7,208},{8,256}... | collective-permute-start | bytes 196616 | tf_op jit(solution)/shard_map/ppermute | solution.py:27
  4.5 3.7 %collective-permute-done = bf16[64,512]{1,0:T(8,128)(2,1)S(1)} collective-permute-done((bf16[64,512]{1,0:T(8,128)(2,1)}, bf16[64,512]{1,0:T(8,128)(2,1)S(1)}, u32[]{:S(2)}, u32[]{:S(2)}) %collective-permute-start) | collective-permute-done | bytes 65568 | tf_op jit(solution)/shard_map/ppermute | solution.py:27
  8.2 35.8 %all_to_all.20.b0 = bf16[8,64,512]{2,1,0:T(8,128)(2,1)S(1)} all-to-all(bf16[8,64,512]{2,1,0:T(8,128)(2,1)S(1)} %broadcast_in_dim.34), channel_id=1, replica_groups={{0,32,144,176,256,288,400,432},{1,97,129,225,257,353,385,481},{2,34,146..., dimensions={0} | all-to-all | bytes 1048576 | tf_op jit(solution)/shard_map/all_to_all | solution.py:38
  44.1 1.9 %collective-permute-start.2 = (bf16[8,64,512]{2,1,0:T(8,128)(2,1)S(1)}, bf16[8,64,512]{2,1,0:T(8,128)(2,1)S(1)}, u32[]{:S(2)}, u32[]{:S(2)}) collective-permute-start(bf16[8,64,512]{2,1,0:T(8,128)(2,1)S(1)} %all_to_all.20.b0), channel_id=1, source_target_pairs={{0,448},{1,49},{2,450},{3,51},{4,452},{5,53},{6,454},{7,55},{8,456... | collective-permute-start | bytes 1572872 | tf_op jit(solution)/shard_map/ppermute | solution.py:27
  46.0 3.4 %collective-permute-start.1 = (bf16[8,64,512]{2,1,0:T(8,128)(2,1)S(1)}, bf16[8,64,512]{2,1,0:T(8,128)(2,1)S(1)}, u32[]{:S(2)}, u32[]{:S(2)}) collective-permute-start(bf16[8,64,512]{2,1,0:T(8,128)(2,1)S(1)} %all_to_all.20.b0), channel_id=1, source_target_pairs={{0,64},{1,17},{2,66},{3,19},{4,68},{5,21},{6,70},{7,23},{8,72},{9,... | collective-permute-start | bytes 1572872 | tf_op jit(solution)/shard_map/ppermute | solution.py:27
  49.4 4.4 %collective-permute-start.4 = (bf16[4,64,512]{2,1,0:T(8,128)(2,1)S(1)}, bf16[4,64,512]{2,1,0:T(8,128)(2,1)S(1)}, u32[]{:S(2)}, u32[]{:S(2)}) collective-permute-start(bf16[4,64,512]{2,1,0:T(8,128)(2,1)S(1)} %get-tuple-element.15), channel_id=1, source_target_pairs={{0,48},{1,449},{2,50},{3,451},{4,52},{5,453},{6,54},{7,455},{8,56}... | collective-permute-start | bytes 786440 | tf_op jit(solution)/shard_map/ppermute | solution.py:27
  53.8 1.9 %collective-permute-start.3 = (bf16[4,64,512]{2,1,0:T(8,128)(2,1)S(1)}, bf16[4,64,512]{2,1,0:T(8,128)(2,1)S(1)}, u32[]{:S(2)}, u32[]{:S(2)}) collective-permute-start(bf16[4,64,512]{2,1,0:T(8,128)(2,1)S(1)} %get-tuple-element.16), channel_id=1, source_target_pairs={{0,16},{1,65},{2,18},{3,67},{4,20},{5,69},{6,22},{7,71},{8,24},{9,... | collective-permute-start | bytes 786440 | tf_op jit(solution)/shard_map/ppermute | solution.py:27
  56.4 0.7 compare_select_fusion.4
  57.1 2.7 %collective-permute-done.4.b4 = bf16[4,64,512]{2,1,0:T(8,128)(2,1)S(1)} collective-permute-done((bf16[4,64,512]{2,1,0:T(8,128)(2,1)S(1)}, bf16[4,64,512]{2,1,0:T(8,128)(2,1)S(1)}, u32[]{:S(2)}, u32[]{:S(2)}) %collective-permute-start.4) | collective-permute-done | bytes 262176 | tf_op jit(solution)/shard_map/ppermute | solution.py:27
  59.9 4.0 %collective-permute-done.3.b3 = bf16[4,64,512]{2,1,0:T(8,128)(2,1)S(1)} collective-permute-done((bf16[4,64,512]{2,1,0:T(8,128)(2,1)S(1)}, bf16[4,64,512]{2,1,0:T(8,128)(2,1)S(1)}, u32[]{:S(2)}, u32[]{:S(2)}) %collective-permute-start.3) | collective-permute-done | bytes 262176 | tf_op jit(solution)/shard_map/ppermute | solution.py:27
  63.9 0.0 collective-permute-done.2.b2
  63.9 0.0 collective-permute-done.1.b1
  63.9 0.0 copy-start
  63.9 1.9 %copy-done = bf16[24,256,256]{2,1,0:T(8,128)(2,1)S(1)} copy-done((bf16[24,256,256]{2,1,0:T(8,128)(2,1)S(1)}, bf16[24,256,256]{2,1,0:T(8,128)(2,1)}, u32[]{:S(2)}) %copy-start) | copy-done | bytes 3145752
  65.8 0.0 copy-start.2
  65.8 2.7 %block_products.2 = (bf16[8,64,512]{2,1,0:T(8,128)(2,1)S(1)}, bf16[8,64,512]{2,1,0:T(8,128)(2,1)S(1)}) custom-call(s32[24]{0:T(128)S(1)} %get-tuple-element.18.place_ref, s32[24]{0:T(128)S(1)} %get-tuple-element.17.row_ref, s32[1]{0:T(128)} %bitcast.1.core_ref, bf16[8,64,512]{2,1,0:T(8,128)(2,1)S(1)} %all_to_all.20.b0, ...), custom_call_target="tpu_custom_call" | custom-call | flops 201326592 | bytes 8388608 | tf_op jit(solution)/shard_map/block_products/pallas_call | solution.py:136
  68.5 0.0 copy-start.1
  68.5 2.9 %collective-permute-start.5 = (bf16[8,64,512]{2,1,0:T(8,128)(2,1)S(1)}, bf16[8,64,512]{2,1,0:T(8,128)(2,1)S(1)}, u32[]{:S(2)}, u32[]{:S(2)}) collective-permute-start(bf16[8,64,512]{2,1,0:T(8,128)(2,1)S(1)} %get-tuple-element.10), channel_id=1, source_target_pairs={{0,1},{1,0},{2,3},{3,2},{4,5},{5,4},{6,7},{7,6},{8,9},{9,8},{10,11... | collective-permute-start | bytes 1572872 | tf_op jit(solution)/shard_map/ppermute | solution.py:27
  71.4 1.5 collective-permute-done.5
  72.9 0.9 add_convert_fusion.1
  73.9 5.3 %all-to-all-start.1 = ((bf16[8,64,512]{2,1,0:T(8,128)(2,1)}), bf16[8,64,512]{2,1,0:T(8,128)(2,1)}, u32[]{:S(2)}, u32[]{:S(2)}) async-start(bf16[8,64,512]{2,1,0:T(8,128)(2,1)} %add_convert_fusion.1), calls=%async_computation.1 | async-start | bytes 1048576 | tf_op jit(solution)/shard_map/all_to_all | solution.py:38
  80.5 16.8 %all-to-all-done.1 = bf16[8,64,512]{2,1,0:T(8,128)(2,1)} async-done(((bf16[8,64,512]{2,1,0:T(8,128)(2,1)}), bf16[8,64,512]{2,1,0:T(8,128)(2,1)}, u32[]{:S(2)}, u32[]{:S(2)}) %all-to-all-start.1) | async-done | bytes 524320 | tf_op jit(solution)/shard_map/all_to_all | solution.py:38
  97.2 1.1 convert_reduce_fusion.1
  98.3 0.0 copy-done.2
  98.4 3.1 %collective-permute-start.6 = (bf16[64,512]{1,0:T(8,128)(2,1)S(1)}, bf16[64,512]{1,0:T(8,128)(2,1)S(1)}, u32[]{:S(2)}, u32[]{:S(2)}) collective-permute-start(bf16[64,512]{1,0:T(8,128)(2,1)S(1)} %fusion.2), channel_id=1, source_target_pairs={{0,0},{1,16},{2,64},{3,80},{4,128},{5,144},{6,192},{7,208},{8,256}... | collective-permute-start | bytes 196616 | tf_op jit(solution)/shard_map/ppermute | solution.py:27
  101.5 4.0 %collective-permute-done.6 = bf16[64,512]{1,0:T(8,128)(2,1)S(1)} collective-permute-done((bf16[64,512]{1,0:T(8,128)(2,1)S(1)}, bf16[64,512]{1,0:T(8,128)(2,1)S(1)}, u32[]{:S(2)}, u32[]{:S(2)}) %collective-permute-start.6) | collective-permute-done | bytes 65568 | tf_op jit(solution)/shard_map/ppermute | solution.py:27
  105.5 29.2 %all_to_all.21.b0 = bf16[8,64,512]{2,1,0:T(8,128)(2,1)S(1)} all-to-all(bf16[8,64,512]{2,1,0:T(8,128)(2,1)S(1)} %broadcast_in_dim.35), channel_id=1, replica_groups={{0,32,144,176,256,288,400,432},{1,97,129,225,257,353,385,481},{2,34,146..., dimensions={0} | all-to-all | bytes 1048576 | tf_op jit(solution)/shard_map/all_to_all | solution.py:38
  134.7 1.9 %collective-permute-start.8 = (bf16[8,64,512]{2,1,0:T(8,128)(2,1)S(1)}, bf16[8,64,512]{2,1,0:T(8,128)(2,1)S(1)}, u32[]{:S(2)}, u32[]{:S(2)}) collective-permute-start(bf16[8,64,512]{2,1,0:T(8,128)(2,1)S(1)} %all_to_all.21.b0), channel_id=1, source_target_pairs={{0,448},{1,49},{2,450},{3,51},{4,452},{5,53},{6,454},{7,55},{8,456... | collective-permute-start | bytes 1572872 | tf_op jit(solution)/shard_map/ppermute | solution.py:27
  136.6 3.4 %collective-permute-start.7 = (bf16[8,64,512]{2,1,0:T(8,128)(2,1)S(1)}, bf16[8,64,512]{2,1,0:T(8,128)(2,1)S(1)}, u32[]{:S(2)}, u32[]{:S(2)}) collective-permute-start(bf16[8,64,512]{2,1,0:T(8,128)(2,1)S(1)} %all_to_all.21.b0), channel_id=1, source_target_pairs={{0,64},{1,17},{2,66},{3,19},{4,68},{5,21},{6,70},{7,23},{8,72},{9,... | collective-permute-start | bytes 1572872 | tf_op jit(solution)/shard_map/ppermute | solution.py:27
  140.0 2.0 %collective-permute-start.10 = (bf16[4,64,512]{2,1,0:T(8,128)(2,1)S(1)}, bf16[4,64,512]{2,1,0:T(8,128)(2,1)S(1)}, u32[]{:S(2)}, u32[]{:S(2)}) collective-permute-start(bf16[4,64,512]{2,1,0:T(8,128)(2,1)S(1)} %get-tuple-element.13), channel_id=1, source_target_pairs={{0,48},{1,449},{2,50},{3,451},{4,52},{5,453},{6,54},{7,455},{8,56}... | collective-permute-start | bytes 786440 | tf_op jit(solution)/shard_map/ppermute | solution.py:27
  142.0 3.2 %collective-permute-start.9 = (bf16[4,64,512]{2,1,0:T(8,128)(2,1)S(1)}, bf16[4,64,512]{2,1,0:T(8,128)(2,1)S(1)}, u32[]{:S(2)}, u32[]{:S(2)}) collective-permute-start(bf16[4,64,512]{2,1,0:T(8,128)(2,1)S(1)} %get-tuple-element.14), channel_id=1, source_target_pairs={{0,16},{1,65},{2,18},{3,67},{4,20},{5,69},{6,22},{7,71},{8,24},{9,... | collective-permute-start | bytes 786440 | tf_op jit(solution)/shard_map/ppermute | solution.py:27
  145.3 3.7 %collective-permute-done.10.b4 = bf16[4,64,512]{2,1,0:T(8,128)(2,1)S(1)} collective-permute-done((bf16[4,64,512]{2,1,0:T(8,128)(2,1)S(1)}, bf16[4,64,512]{2,1,0:T(8,128)(2,1)S(1)}, u32[]{:S(2)}, u32[]{:S(2)}) %collective-permute-start.10) | collective-permute-done | bytes 262176 | tf_op jit(solution)/shard_map/ppermute | solution.py:27
  149.0 4.2 %collective-permute-done.9.b3 = bf16[4,64,512]{2,1,0:T(8,128)(2,1)S(1)} collective-permute-done((bf16[4,64,512]{2,1,0:T(8,128)(2,1)S(1)}, bf16[4,64,512]{2,1,0:T(8,128)(2,1)S(1)}, u32[]{:S(2)}, u32[]{:S(2)}) %collective-permute-start.9) | collective-permute-done | bytes 262176 | tf_op jit(solution)/shard_map/ppermute | solution.py:27
  153.2 0.0 collective-permute-done.8.b2
  153.2 0.0 collective-permute-done.7.b1
  153.2 0.0 copy-done.1
  153.2 2.7 %block_products.3 = (bf16[8,64,512]{2,1,0:T(8,128)(2,1)S(1)}, bf16[8,64,512]{2,1,0:T(8,128)(2,1)S(1)}) custom-call(s32[24]{0:T(128)S(1)} %get-tuple-element.18.place_ref, s32[24]{0:T(128)S(1)} %get-tuple-element.17.row_ref, s32[1]{0:T(128)} %bitcast.1.core_ref, bf16[8,64,512]{2,1,0:T(8,128)(2,1)S(1)} %all_to_all.21.b0, ...), custom_call_target="tpu_custom_call" | custom-call | flops 201326592 | bytes 8388608 | tf_op jit(solution)/shard_map/block_products/pallas_call | solution.py:136
  156.0 3.0 %collective-permute-start.11 = (bf16[8,64,512]{2,1,0:T(8,128)(2,1)S(1)}, bf16[8,64,512]{2,1,0:T(8,128)(2,1)S(1)}, u32[]{:S(2)}, u32[]{:S(2)}) collective-permute-start(bf16[8,64,512]{2,1,0:T(8,128)(2,1)S(1)} %get-tuple-element.12), channel_id=1, source_target_pairs={{0,1},{1,0},{2,3},{3,2},{4,5},{5,4},{6,7},{7,6},{8,9},{9,8},{10,11... | collective-permute-start | bytes 1572872 | tf_op jit(solution)/shard_map/ppermute | solution.py:27
  159.0 1.5 collective-permute-done.11
  160.5 0.1 add_convert_fusion
  160.7 20.4 %all_to_all.22 = bf16[8,64,512]{2,1,0:T(8,128)(2,1)S(1)} all-to-all(bf16[8,64,512]{2,1,0:T(8,128)(2,1)S(1)} %add_convert_fusion), channel_id=1, replica_groups={{0,2,4,6,8,10,12,14},{1,3,5,7,9,11,13,15},{16,18,20,22,24,26,28,30},{17..., dimensions={0} | all-to-all | bytes 1048576 | tf_op jit(solution)/shard_map/all_to_all | solution.py:38
  181.1 0.1 convert_reduce_fusion
  181.1 0.7 fusion.3
  (5 shorter events, 0.2 us)
Async XLA Ops:
  0.0 8.2 %collective-permute-start = (bf16[64,512]{1,0:T(8,128)(2,1)}, bf16[64,512]{1,0:T(8,128)(2,1)S(1)}, u32[]{:S(2)}, u32[]{:S(2)}) collective-permute-start(bf16[64,512]{1,0:T(8,128)(2,1)} %param.7), channel_id=1, source_target_pairs={{0,0},{1,16},{2,64},{3,80},{4,128},{5,144},{6,192},{7,208},{8,256}... | collective-permute-start | bytes 196616 | tf_op jit(solution)/shard_map/ppermute | solution.py:27
  44.1 19.8 %collective-permute-start.2 = (bf16[8,64,512]{2,1,0:T(8,128)(2,1)S(1)}, bf16[8,64,512]{2,1,0:T(8,128)(2,1)S(1)}, u32[]{:S(2)}, u32[]{:S(2)}) collective-permute-start(bf16[8,64,512]{2,1,0:T(8,128)(2,1)S(1)} %all_to_all.20.b0), channel_id=1, source_target_pairs={{0,448},{1,49},{2,450},{3,51},{4,452},{5,53},{6,454},{7,55},{8,456... | collective-permute-start | bytes 1572872 | tf_op jit(solution)/shard_map/ppermute | solution.py:27
  46.0 17.9 %collective-permute-start.1 = (bf16[8,64,512]{2,1,0:T(8,128)(2,1)S(1)}, bf16[8,64,512]{2,1,0:T(8,128)(2,1)S(1)}, u32[]{:S(2)}, u32[]{:S(2)}) collective-permute-start(bf16[8,64,512]{2,1,0:T(8,128)(2,1)S(1)} %all_to_all.20.b0), channel_id=1, source_target_pairs={{0,64},{1,17},{2,66},{3,19},{4,68},{5,21},{6,70},{7,23},{8,72},{9,... | collective-permute-start | bytes 1572872 | tf_op jit(solution)/shard_map/ppermute | solution.py:27
  49.4 10.5 %collective-permute-start.4 = (bf16[4,64,512]{2,1,0:T(8,128)(2,1)S(1)}, bf16[4,64,512]{2,1,0:T(8,128)(2,1)S(1)}, u32[]{:S(2)}, u32[]{:S(2)}) collective-permute-start(bf16[4,64,512]{2,1,0:T(8,128)(2,1)S(1)} %get-tuple-element.15), channel_id=1, source_target_pairs={{0,48},{1,449},{2,50},{3,451},{4,52},{5,453},{6,54},{7,455},{8,56}... | collective-permute-start | bytes 786440 | tf_op jit(solution)/shard_map/ppermute | solution.py:27
  53.8 10.0 %collective-permute-start.3 = (bf16[4,64,512]{2,1,0:T(8,128)(2,1)S(1)}, bf16[4,64,512]{2,1,0:T(8,128)(2,1)S(1)}, u32[]{:S(2)}, u32[]{:S(2)}) collective-permute-start(bf16[4,64,512]{2,1,0:T(8,128)(2,1)S(1)} %get-tuple-element.16), channel_id=1, source_target_pairs={{0,16},{1,65},{2,18},{3,67},{4,20},{5,69},{6,22},{7,71},{8,24},{9,... | collective-permute-start | bytes 786440 | tf_op jit(solution)/shard_map/ppermute | solution.py:27
  63.9 1.9 %copy-start = (bf16[24,256,256]{2,1,0:T(8,128)(2,1)S(1)}, bf16[24,256,256]{2,1,0:T(8,128)(2,1)}, u32[]{:S(2)}) copy-start(bf16[24,256,256]{2,1,0:T(8,128)(2,1)} %tiles_hbm.3) | copy-start | bytes 9437188
  65.8 32.6 %copy-start.2 = (bf16[64,512]{1,0:T(8,128)(2,1)S(1)}, bf16[64,512]{1,0:T(8,128)(2,1)}, u32[]{:S(2)}) copy-start(bf16[64,512]{1,0:T(8,128)(2,1)} %param.7) | copy-start | bytes 196612
  68.5 84.8 %copy-start.1 = (bf16[24,256,256]{2,1,0:T(8,128)(2,1)S(1)}, bf16[24,256,256]{2,1,0:T(8,128)(2,1)}, u32[]{:S(2)}) copy-start(bf16[24,256,256]{2,1,0:T(8,128)(2,1)} %tiles_hbm.3) | copy-start | bytes 9437188
  68.5 4.4 %collective-permute-start.5 = (bf16[8,64,512]{2,1,0:T(8,128)(2,1)S(1)}, bf16[8,64,512]{2,1,0:T(8,128)(2,1)S(1)}, u32[]{:S(2)}, u32[]{:S(2)}) collective-permute-start(bf16[8,64,512]{2,1,0:T(8,128)(2,1)S(1)} %get-tuple-element.10), channel_id=1, source_target_pairs={{0,1},{1,0},{2,3},{3,2},{4,5},{5,4},{6,7},{7,6},{8,9},{9,8},{10,11... | collective-permute-start | bytes 1572872 | tf_op jit(solution)/shard_map/ppermute | solution.py:27
  73.9 23.3 %all-to-all-start.1 = ((bf16[8,64,512]{2,1,0:T(8,128)(2,1)}), bf16[8,64,512]{2,1,0:T(8,128)(2,1)}, u32[]{:S(2)}, u32[]{:S(2)}) async-start(bf16[8,64,512]{2,1,0:T(8,128)(2,1)} %add_convert_fusion.1), calls=%async_computation.1 | async-start | bytes 1048576 | tf_op jit(solution)/shard_map/all_to_all | solution.py:38
  98.4 7.1 %collective-permute-start.6 = (bf16[64,512]{1,0:T(8,128)(2,1)S(1)}, bf16[64,512]{1,0:T(8,128)(2,1)S(1)}, u32[]{:S(2)}, u32[]{:S(2)}) collective-permute-start(bf16[64,512]{1,0:T(8,128)(2,1)S(1)} %fusion.2), channel_id=1, source_target_pairs={{0,0},{1,16},{2,64},{3,80},{4,128},{5,144},{6,192},{7,208},{8,256}... | collective-permute-start | bytes 196616 | tf_op jit(solution)/shard_map/ppermute | solution.py:27
  134.7 18.6 %collective-permute-start.8 = (bf16[8,64,512]{2,1,0:T(8,128)(2,1)S(1)}, bf16[8,64,512]{2,1,0:T(8,128)(2,1)S(1)}, u32[]{:S(2)}, u32[]{:S(2)}) collective-permute-start(bf16[8,64,512]{2,1,0:T(8,128)(2,1)S(1)} %all_to_all.21.b0), channel_id=1, source_target_pairs={{0,448},{1,49},{2,450},{3,51},{4,452},{5,53},{6,454},{7,55},{8,456... | collective-permute-start | bytes 1572872 | tf_op jit(solution)/shard_map/ppermute | solution.py:27
  136.6 16.6 %collective-permute-start.7 = (bf16[8,64,512]{2,1,0:T(8,128)(2,1)S(1)}, bf16[8,64,512]{2,1,0:T(8,128)(2,1)S(1)}, u32[]{:S(2)}, u32[]{:S(2)}) collective-permute-start(bf16[8,64,512]{2,1,0:T(8,128)(2,1)S(1)} %all_to_all.21.b0), channel_id=1, source_target_pairs={{0,64},{1,17},{2,66},{3,19},{4,68},{5,21},{6,70},{7,23},{8,72},{9,... | collective-permute-start | bytes 1572872 | tf_op jit(solution)/shard_map/ppermute | solution.py:27
  140.0 9.0 %collective-permute-start.10 = (bf16[4,64,512]{2,1,0:T(8,128)(2,1)S(1)}, bf16[4,64,512]{2,1,0:T(8,128)(2,1)S(1)}, u32[]{:S(2)}, u32[]{:S(2)}) collective-permute-start(bf16[4,64,512]{2,1,0:T(8,128)(2,1)S(1)} %get-tuple-element.13), channel_id=1, source_target_pairs={{0,48},{1,449},{2,50},{3,451},{4,52},{5,453},{6,54},{7,455},{8,56}... | collective-permute-start | bytes 786440 | tf_op jit(solution)/shard_map/ppermute | solution.py:27
  142.0 11.2 %collective-permute-start.9 = (bf16[4,64,512]{2,1,0:T(8,128)(2,1)S(1)}, bf16[4,64,512]{2,1,0:T(8,128)(2,1)S(1)}, u32[]{:S(2)}, u32[]{:S(2)}) collective-permute-start(bf16[4,64,512]{2,1,0:T(8,128)(2,1)S(1)} %get-tuple-element.14), channel_id=1, source_target_pairs={{0,16},{1,65},{2,18},{3,67},{4,20},{5,69},{6,22},{7,71},{8,24},{9,... | collective-permute-start | bytes 786440 | tf_op jit(solution)/shard_map/ppermute | solution.py:27
  156.0 4.6 %collective-permute-start.11 = (bf16[8,64,512]{2,1,0:T(8,128)(2,1)S(1)}, bf16[8,64,512]{2,1,0:T(8,128)(2,1)S(1)}, u32[]{:S(2)}, u32[]{:S(2)}) collective-permute-start(bf16[8,64,512]{2,1,0:T(8,128)(2,1)S(1)} %get-tuple-element.12), channel_id=1, source_target_pairs={{0,1},{1,0},{2,3},{3,2},{4,5},{5,4},{6,7},{7,6},{8,9},{9,8},{10,11... | collective-permute-start | bytes 1572872 | tf_op jit(solution)/shard_map/ppermute | solution.py:27

commit v2 on v1

--- a/solution.py
+++ b/solution.py
@@ -47,7 +47,7 @@
 
 
 def to_column_plane(z, x, y, c):
-    return (y, (x % 2) * 2 + c, z, x // 2)
+    return (2 * z + 4 - y, x if c == 0 else 3 - x, z, x // 2)
 
 
 def along(sign):
@@ -62,19 +62,18 @@
     return (z, x, y, 1 - c)
 
 
-def column_panel(piece):
-    mine = permute(piece, to_column_plane)
+def column_panel(mine):
     bundle = exchange(jnp.broadcast_to(mine[None], (8,) + mine.shape), CLASSES)
     below = permute(bundle, along(1))
     above = permute(bundle, along(-1))
-    first = permute(bundle[:4], across(1))
-    second = permute(bundle[4:], across(-1))
-    return bundle, below, above, first, second
-
-
-def block_places(tile_col, z, x, c):
-    from_z = (tile_col % 32) // 4
-    from_x = (tile_col // 32) * 2 + (tile_col // 2) % 2
+    beside = permute(bundle, across(1))
+    return bundle, below, above, beside
+
+
+def block_places(tile_col, z, x, y, c):
+    owner_x = 2 * c + tile_col // 32
+    from_z = (2 * y + 4 - (tile_col % 32) // 4) % 8
+    from_x = jnp.where((tile_col // 2) % 2 == 0, owner_x, 3 - owner_x)
     theirs = jnp.where(c == 0, from_z + 2 * from_x, from_x + 2 * from_z)
     own = jnp.where(c == 0, z + 2 * x, x + 2 * z)
     member = jnp.where(c == 0, (from_z // 2) * 2 + from_x // 2, from_z)
@@ -83,37 +82,42 @@
     return (start + member) * 2 + tile_col % 2
 
 
+def load_kernel(tiles_hbm, tiles_ref, sem):
+    load = pltpu.make_async_copy(tiles_hbm, tiles_ref, sem)
+    load.start()
+    load.wait()
+
+
+def load_tiles(tiles):
+    return pl.pallas_call(
+        load_kernel,
+        out_shape=jax.ShapeDtypeStruct(tiles.shape, tiles.dtype),
+        in_specs=[pl.BlockSpec(memory_space=pl.ANY)],
+        out_specs=pl.BlockSpec(memory_space=pl.ANY),
+        scratch_shapes=[pltpu.SemaphoreType.DMA],
+        compiler_params=pltpu.CompilerParams(vmem_limit_bytes=16 * 1024 * 1024),
+        name="load_tiles",
+    )(tiles)
+
+
 def product_kernel(
-    place_ref, row_ref, core_ref, b0, b1, b2, b3, b4, tiles_hbm,
-    keep_ref, give_ref, panel, tiles, total, panel_sems, tile_sems,
+    place_ref, row_ref, core_ref, b0, b1, b2, b3, tiles, keep_ref, give_ref, total
 ):
-    chunk = SLOTS // 4
-    loads = []
-    for index, (source, start, size) in enumerate(
-        ((b0, 0, 8), (b1, 8, 8), (b2, 16, 8), (b3, 24, 4), (b4, 28, 4))
-    ):
-        loads.append(
-            pltpu.make_async_copy(source, panel.at[pl.ds(start, size)], panel_sems.at[index])
-        )
-    tile_loads = []
-    for index in range(4):
-        part = pl.ds(index * chunk, chunk)
-        tile_loads.append(
-            pltpu.make_async_copy(tiles_hbm.at[part], tiles.at[part], tile_sems.at[index])
-        )
-    for load in loads + tile_loads:
-        load.start()
     total[...] = jnp.zeros_like(total)
-    for load in loads:
-        load.wait()
-    for index in range(4):
-        tile_loads[index].wait()
-        slots = range(index * chunk, (index + 1) * chunk)
+    chunk = 6
+    for first in range(0, SLOTS, chunk):
+        slots = range(first, first + chunk)
         products = []
         for slot in slots:
             place = place_ref[slot]
-            half = pl.multiple_of((place % 2) * TB, TB)
-            block = panel[place // 2, :, pl.ds(half, TB)]
+            part = place // 16
+            member = (place // 2) % 8
+            columns = pl.ds(pl.multiple_of((place % 2) * TB, TB), TB)
+            block = jnp.where(
+                part < 2,
+                jnp.where(part == 0, b0[member, :, columns], b1[member, :, columns]),
+                jnp.where(part == 2, b2[member, :, columns], b3[member, :, columns]),
+            )
             products.append(
                 lax.dot_general(
                     block, tiles[slot], (((1,), (1,)), ((), ())),
@@ -137,15 +141,9 @@
         product_kernel,
         out_shape=(half_panel, half_panel),
         in_specs=[pl.BlockSpec(memory_space=pltpu.SMEM)] * 3
-        + [pl.BlockSpec(memory_space=pl.ANY)] * 6,
+        + [pl.BlockSpec(memory_space=pltpu.VMEM)] * 5,
         out_specs=(pl.BlockSpec(memory_space=pltpu.VMEM),) * 2,
-        scratch_shapes=[
-            pltpu.VMEM((32, NV, PIECE), jnp.bfloat16),
-            pltpu.VMEM((SLOTS, TB, TB), jnp.bfloat16),
-            pltpu.VMEM((BR + 1, NV, TB), jnp.float32),
-            pltpu.SemaphoreType.DMA((5,)),
-            pltpu.SemaphoreType.DMA((4,)),
-        ],
+        scratch_shapes=[pltpu.VMEM((BR + 1, NV, TB), jnp.float32)],
         compiler_params=pltpu.CompilerParams(vmem_limit_bytes=24 * 1024 * 1024),
         cost_estimate=pl.CostEstimate(
             flops=2 * SLOTS * NV * TB * TB, bytes_accessed=8 * 1024 * 1024, transcendentals=0
@@ -154,6 +152,11 @@
     )(places, rows, core, *parts, tiles)
 
 
+def line_sum(keep, taken):
+    pair = (keep.astype(jnp.float32) + taken.astype(jnp.float32)).astype(jnp.bfloat16)
+    return jnp.sum(exchange(pair, LINES).astype(jnp.float32), axis=0)
+
+
 def recurrence(sums, current, previous, center, half, step):
     shifted = (sums - center * current.astype(jnp.float32)) / half
     if step == 0:
@@ -165,18 +168,23 @@
     center = (upper[0] + lower[0]) / 2.0
     half = (upper[0] - lower[0]) / 2.0
     row, col = lax.axis_index("row"), lax.axis_index("col")
-    z, x, core = row // NX, row % NX, col % NC
-    places = block_places(tile_col, z, x, core)
+    z, x, y, core = row // NX, row % NX, col // NC, col % NC
+    places = block_places(tile_col, z, x, y, core)
     used = jnp.arange(SLOTS, dtype=jnp.int32) < tile_count[0]
     rows = jnp.where(used, tile_row, BR)
     core_ref = core.astype(jnp.int32)[None]
     current = previous = vectors
+    moved = permute(current, to_column_plane)
+    moved, tiles, places, rows, center, half = lax.optimization_barrier(
+        (moved, load_tiles(tiles), places, rows, center, half)
+    )
     for step in range(DEGREE):
-        parts = column_panel(current)
+        if step > 0:
+            moved = permute(current, to_column_plane)
+        parts = column_panel(moved)
         keep, give = local_product(parts, tiles, places, rows, core_ref)
         taken = permute(give, other_core)
-        pair = (keep.astype(jnp.float32) + taken.astype(jnp.float32)).astype(jnp.bfloat16)
-        sums = jnp.sum(exchange(pair, LINES).astype(jnp.float32), axis=0)
+        sums = line_sum(keep, taken)
         following = recurrence(sums, current, previous, center, half, step)
         previous, current = (current, following)
     return current

time: 183 us -> 173 us (0.945)
  waiting for transfers between devices: 42.1 us -> 26.3 us
  starting transfers between devices: 40.9 us -> 51.1 us
  other arithmetic: 3.7 us -> 1.84 us
    all_to_all x1 -> x0, waiting for transfers between devices: 16.8 us -> none  [exchange(): lax.all_to_all(value, AXES, 0, 0, axis_index_groups=groups, tiled=True)]
    ppermute x12 -> x10, starting transfers between devices: 35.7 us -> 51.1 us  [permute(): lax.ppermute(value, AXES, [(number(*p), number(*move(*p))) for p in PLACES])]
    all_to_all x1 -> x0, starting transfers between devices: 5.26 us -> none  [exchange(): lax.all_to_all(value, AXES, 0, 0, axis_index_groups=groups, tiled=True)]
    ppermute x12 -> x10, waiting for transfers between devices: 25.4 us -> 26.3 us  [permute(): lax.ppermute(value, AXES, [(number(*p), number(*move(*p))) for p in PLACES])]
    all_to_all x3 -> x4, blocking collectives: 85.4 us -> 85 us  [exchange(): lax.all_to_all(value, AXES, 0, 0, axis_index_groups=groups, tiled=True)]
  transfers between devices with their start and end apart: 13 -> 10, of which waited for: 9 -> 9; matrix products, arithmetic and copies ran while one was open for 0% -> 0% of each run, Pallas kernels for 0% -> 0%
where the time goes in v2:
time: 173 us; the launch traced here: 172 us
  blocking collectives  85 us (49%)
  starting transfers between devices  51.1 us (30%)
  waiting for transfers between devices  26.3 us (15%)
  Pallas kernels  3.89 us (2%)
  between operations  2.16 us (1%)
  local copies, waits for them, and re-layouts  1.96 us (1%)
  other arithmetic  1.84 us (1%)
    all_to_all x4, blocking collectives, exchange(): lax.all_to_all(value, AXES, 0, 0, axis_index_groups=groups, tiled=True)  85 us
    ppermute x10, starting transfers between devices, permute(): lax.ppermute(value, AXES, [(number(*p), number(*move(*p))) for p in PLACES])  51.1 us
    ppermute x10, waiting for transfers between devices, permute(): lax.ppermute(value, AXES, [(number(*p), number(*move(*p))) for p in PLACES])  26.3 us
    pallas_call x2, Pallas kernels, local_product(): pl.pallas_call(product_kernel, out_shape=(half_panel, half_panel), in_spe...  3.67 us
  transfers between devices with their start and end apart: 10, of which 9 were waited for; matrix products, arithmetic and copies ran while one was open for 0% of the time, Pallas kernels for 0%

profile of v2, /device:TPU:1, one launch (start us, length us, event | category | flops | bytes accessed | tf_op | source)
XLA Modules:
  0.0 172.3 jit_solution(15670676649466317294)
XLA Ops:
  0.0 14.2 %collective-permute-start = (bf16[64,512]{1,0:T(8,128)(2,1)}, bf16[64,512]{1,0:T(8,128)(2,1)S(1)}, u32[]{:S(2)}, u32[]{:S(2)}) collective-permute-start(bf16[64,512]{1,0:T(8,128)(2,1)} %param.7), channel_id=1, source_target_pairs={{0,256},{1,304},{2,192},{3,240},{4,128},{5,176},{6,64},{7,112},{8,... | collective-permute-start | bytes 196616 | tf_op jit(solution)/shard_map/ppermute | solution.py:27
  14.9 0.7 compare_select_fusion.6
  16.9 0.0 copy-start
  16.9 1.9 %copy-done = bf16[24,256,256]{2,1,0:T(8,128)(2,1)S(1)} copy-done((bf16[24,256,256]{2,1,0:T(8,128)(2,1)S(1)}, bf16[24,256,256]{2,1,0:T(8,128)(2,1)}, u32[]{:S(2)}) %copy-start) | copy-done | bytes 3145752
  18.8 0.2 load_tiles.1.tiles
  19.0 0.0 collective-permute-done
  19.1 26.2 %all_to_all.20.b0 = bf16[8,64,512]{2,1,0:T(8,128)(2,1)S(1)} all-to-all(bf16[8,64,512]{2,1,0:T(8,128)(2,1)S(1)} %broadcast_in_dim.31), channel_id=1, replica_groups={{0,32,144,176,256,288,400,432},{1,97,129,225,257,353,385,481},{2,34,146..., dimensions={0} | all-to-all | bytes 1048576 | tf_op jit(solution)/shard_map/all_to_all | solution.py:38
  45.3 1.9 %collective-permute-start.3 = (bf16[8,64,512]{2,1,0:T(8,128)(2,1)S(1)}, bf16[8,64,512]{2,1,0:T(8,128)(2,1)S(1)}, u32[]{:S(2)}, u32[]{:S(2)}) collective-permute-start(bf16[8,64,512]{2,1,0:T(8,128)(2,1)S(1)} %all_to_all.20.b0), channel_id=1, source_target_pairs={{0,16},{1,65},{2,18},{3,67},{4,20},{5,69},{6,22},{7,71},{8,24},{9,... | collective-permute-start | bytes 1572872 | tf_op jit(solution)/shard_map/ppermute | solution.py:27
  47.2 2.7 %collective-permute-start.2 = (bf16[8,64,512]{2,1,0:T(8,128)(2,1)S(1)}, bf16[8,64,512]{2,1,0:T(8,128)(2,1)S(1)}, u32[]{:S(2)}, u32[]{:S(2)}) collective-permute-start(bf16[8,64,512]{2,1,0:T(8,128)(2,1)S(1)} %all_to_all.20.b0), channel_id=1, source_target_pairs={{0,448},{1,49},{2,450},{3,51},{4,452},{5,53},{6,454},{7,55},{8,456... | collective-permute-start | bytes 1572872 | tf_op jit(solution)/shard_map/ppermute | solution.py:27
  49.9 2.6 %collective-permute-start.1 = (bf16[8,64,512]{2,1,0:T(8,128)(2,1)S(1)}, bf16[8,64,512]{2,1,0:T(8,128)(2,1)S(1)}, u32[]{:S(2)}, u32[]{:S(2)}) collective-permute-start(bf16[8,64,512]{2,1,0:T(8,128)(2,1)S(1)} %all_to_all.20.b0), channel_id=1, source_target_pairs={{0,64},{1,17},{2,66},{3,19},{4,68},{5,21},{6,70},{7,23},{8,72},{9,... | collective-permute-start | bytes 1572872 | tf_op jit(solution)/shard_map/ppermute | solution.py:27
  52.5 4.2 %collective-permute-done.3.b3 = bf16[8,64,512]{2,1,0:T(8,128)(2,1)S(1)} collective-permute-done((bf16[8,64,512]{2,1,0:T(8,128)(2,1)S(1)}, bf16[8,64,512]{2,1,0:T(8,128)(2,1)S(1)}, u32[]{:S(2)}, u32[]{:S(2)}) %collective-permute-start.3) | collective-permute-done | bytes 524320 | tf_op jit(solution)/shard_map/ppermute | solution.py:27
  56.7 0.7 collective-permute-done.2.b2
  57.4 5.8 %collective-permute-done.1.b1 = bf16[8,64,512]{2,1,0:T(8,128)(2,1)S(1)} collective-permute-done((bf16[8,64,512]{2,1,0:T(8,128)(2,1)S(1)}, bf16[8,64,512]{2,1,0:T(8,128)(2,1)S(1)}, u32[]{:S(2)}, u32[]{:S(2)}) %collective-permute-start.1) | collective-permute-done | bytes 524320 | tf_op jit(solution)/shard_map/ppermute | solution.py:27
  63.2 0.0 copy-start.1
  63.2 1.8 %block_products.2 = (bf16[8,64,512]{2,1,0:T(8,128)(2,1)S(1)}, bf16[8,64,512]{2,1,0:T(8,128)(2,1)S(1)}) custom-call(s32[24]{0:T(128)S(1)} %get-tuple-element.15.place_ref, s32[24]{0:T(128)S(1)} %get-tuple-element.16.row_ref, s32[1]{0:T(128)} %bitcast.3.core_ref, bf16[8,64,512]{2,1,0:T(8,128)(2,1)S(1)} %all_to_all.20.b0, ...), custom_call_target="tpu_custom_call" | custom-call | flops 201326592 | bytes 8388608 | tf_op jit(solution)/shard_map/block_products/pallas_call | solution.py:140
  65.0 2.4 %collective-permute-start.4 = (bf16[8,64,512]{2,1,0:T(8,128)(2,1)S(1)}, bf16[8,64,512]{2,1,0:T(8,128)(2,1)S(1)}, u32[]{:S(2)}, u32[]{:S(2)}) collective-permute-start(bf16[8,64,512]{2,1,0:T(8,128)(2,1)S(1)} %get-tuple-element.20), channel_id=1, source_target_pairs={{0,1},{1,0},{2,3},{3,2},{4,5},{5,4},{6,7},{7,6},{8,9},{9,8},{10,11... | collective-permute-start | bytes 1572872 | tf_op jit(solution)/shard_map/ppermute | solution.py:27
  67.4 1.5 collective-permute-done.4
  68.9 0.1 add_convert_fusion.1
  69.1 20.8 %all_to_all.21 = bf16[8,64,512]{2,1,0:T(8,128)(2,1)S(1)} all-to-all(bf16[8,64,512]{2,1,0:T(8,128)(2,1)S(1)} %add_convert_fusion.1), channel_id=1, replica_groups={{0,2,4,6,8,10,12,14},{1,3,5,7,9,11,13,15},{16,18,20,22,24,26,28,30},{17..., dimensions={0} | all-to-all | bytes 1048576 | tf_op jit(solution)/shard_map/all_to_all | solution.py:38
  89.9 0.1 convert_reduce_fusion.1
  89.9 0.0 copy-done.1
  90.0 9.0 %collective-permute-start.5 = (bf16[64,512]{1,0:T(8,128)(2,1)S(1)}, bf16[64,512]{1,0:T(8,128)(2,1)S(1)}, u32[]{:S(2)}, u32[]{:S(2)}) collective-permute-start(bf16[64,512]{1,0:T(8,128)(2,1)S(1)} %fusion.2), channel_id=1, source_target_pairs={{0,256},{1,304},{2,192},{3,240},{4,128},{5,176},{6,64},{7,112},{8,... | collective-permute-start | bytes 196616 | tf_op jit(solution)/shard_map/ppermute | solution.py:27
  98.9 3.3 %collective-permute-done.5 = bf16[64,512]{1,0:T(8,128)(2,1)S(1)} collective-permute-done((bf16[64,512]{1,0:T(8,128)(2,1)S(1)}, bf16[64,512]{1,0:T(8,128)(2,1)S(1)}, u32[]{:S(2)}, u32[]{:S(2)}) %collective-permute-start.5) | collective-permute-done | bytes 65568 | tf_op jit(solution)/shard_map/ppermute | solution.py:27
  102.3 17.7 %all_to_all.22.b0 = bf16[8,64,512]{2,1,0:T(8,128)(2,1)S(1)} all-to-all(bf16[8,64,512]{2,1,0:T(8,128)(2,1)S(1)} %broadcast_in_dim.32), channel_id=1, replica_groups={{0,32,144,176,256,288,400,432},{1,97,129,225,257,353,385,481},{2,34,146..., dimensions={0} | all-to-all | bytes 1048576 | tf_op jit(solution)/shard_map/all_to_all | solution.py:38
  120.0 11.2 %collective-permute-start.8 = (bf16[8,64,512]{2,1,0:T(8,128)(2,1)S(1)}, bf16[8,64,512]{2,1,0:T(8,128)(2,1)S(1)}, u32[]{:S(2)}, u32[]{:S(2)}) collective-permute-start(bf16[8,64,512]{2,1,0:T(8,128)(2,1)S(1)} %all_to_all.22.b0), channel_id=1, source_target_pairs={{0,16},{1,65},{2,18},{3,67},{4,20},{5,69},{6,22},{7,71},{8,24},{9,... | collective-permute-start | bytes 1572872 | tf_op jit(solution)/shard_map/ppermute | solution.py:27
  131.2 1.9 %collective-permute-start.7 = (bf16[8,64,512]{2,1,0:T(8,128)(2,1)S(1)}, bf16[8,64,512]{2,1,0:T(8,128)(2,1)S(1)}, u32[]{:S(2)}, u32[]{:S(2)}) collective-permute-start(bf16[8,64,512]{2,1,0:T(8,128)(2,1)S(1)} %all_to_all.22.b0), channel_id=1, source_target_pairs={{0,448},{1,49},{2,450},{3,51},{4,452},{5,53},{6,454},{7,55},{8,456... | collective-permute-start | bytes 1572872 | tf_op jit(solution)/shard_map/ppermute | solution.py:27
  133.1 3.4 %collective-permute-start.6 = (bf16[8,64,512]{2,1,0:T(8,128)(2,1)S(1)}, bf16[8,64,512]{2,1,0:T(8,128)(2,1)S(1)}, u32[]{:S(2)}, u32[]{:S(2)}) collective-permute-start(bf16[8,64,512]{2,1,0:T(8,128)(2,1)S(1)} %all_to_all.22.b0), channel_id=1, source_target_pairs={{0,64},{1,17},{2,66},{3,19},{4,68},{5,21},{6,70},{7,23},{8,72},{9,... | collective-permute-start | bytes 1572872 | tf_op jit(solution)/shard_map/ppermute | solution.py:27
  136.5 0.8 collective-permute-done.8.b3
  137.3 4.1 %collective-permute-done.7.b2 = bf16[8,64,512]{2,1,0:T(8,128)(2,1)S(1)} collective-permute-done((bf16[8,64,512]{2,1,0:T(8,128)(2,1)S(1)}, bf16[8,64,512]{2,1,0:T(8,128)(2,1)S(1)}, u32[]{:S(2)}, u32[]{:S(2)}) %collective-permute-start.7) | collective-permute-done | bytes 524320 | tf_op jit(solution)/shard_map/ppermute | solution.py:27
  141.4 4.0 %collective-permute-done.6.b1 = bf16[8,64,512]{2,1,0:T(8,128)(2,1)S(1)} collective-permute-done((bf16[8,64,512]{2,1,0:T(8,128)(2,1)S(1)}, bf16[8,64,512]{2,1,0:T(8,128)(2,1)S(1)}, u32[]{:S(2)}, u32[]{:S(2)}) %collective-permute-start.6) | collective-permute-done | bytes 524320 | tf_op jit(solution)/shard_map/ppermute | solution.py:27
  145.4 1.8 %block_products.3 = (bf16[8,64,512]{2,1,0:T(8,128)(2,1)S(1)}, bf16[8,64,512]{2,1,0:T(8,128)(2,1)S(1)}) custom-call(s32[24]{0:T(128)S(1)} %get-tuple-element.15.place_ref, s32[24]{0:T(128)S(1)} %get-tuple-element.16.row_ref, s32[1]{0:T(128)} %bitcast.3.core_ref, bf16[8,64,512]{2,1,0:T(8,128)(2,1)S(1)} %all_to_all.22.b0, ...), custom_call_target="tpu_custom_call" | custom-call | flops 201326592 | bytes 8388608 | tf_op jit(solution)/shard_map/block_products/pallas_call | solution.py:140
  147.2 1.9 %collective-permute-start.9 = (bf16[8,64,512]{2,1,0:T(8,128)(2,1)S(1)}, bf16[8,64,512]{2,1,0:T(8,128)(2,1)S(1)}, u32[]{:S(2)}, u32[]{:S(2)}) collective-permute-start(bf16[8,64,512]{2,1,0:T(8,128)(2,1)S(1)} %get-tuple-element.24), channel_id=1, source_target_pairs={{0,1},{1,0},{2,3},{3,2},{4,5},{5,4},{6,7},{7,6},{8,9},{9,8},{10,11... | collective-permute-start | bytes 1572872 | tf_op jit(solution)/shard_map/ppermute | solution.py:27
  149.1 1.9 %collective-permute-done.9 = bf16[8,64,512]{2,1,0:T(8,128)(2,1)S(1)} collective-permute-done((bf16[8,64,512]{2,1,0:T(8,128)(2,1)S(1)}, bf16[8,64,512]{2,1,0:T(8,128)(2,1)S(1)}, u32[]{:S(2)}, u32[]{:S(2)}) %collective-permute-start.9) | collective-permute-done | bytes 524320 | tf_op jit(solution)/shard_map/ppermute | solution.py:27
  151.0 0.1 add_convert_fusion
  151.2 20.4 %all_to_all.23 = bf16[8,64,512]{2,1,0:T(8,128)(2,1)S(1)} all-to-all(bf16[8,64,512]{2,1,0:T(8,128)(2,1)S(1)} %add_convert_fusion), channel_id=1, replica_groups={{0,2,4,6,8,10,12,14},{1,3,5,7,9,11,13,15},{16,18,20,22,24,26,28,30},{17..., dimensions={0} | all-to-all | bytes 1048576 | tf_op jit(solution)/shard_map/all_to_all | solution.py:38
  171.6 0.1 convert_reduce_fusion
  171.6 0.7 fusion.3
  (3 shorter events, 0.1 us)
Async XLA Ops:
  0.0 19.0 %collective-permute-start = (bf16[64,512]{1,0:T(8,128)(2,1)}, bf16[64,512]{1,0:T(8,128)(2,1)S(1)}, u32[]{:S(2)}, u32[]{:S(2)}) collective-permute-start(bf16[64,512]{1,0:T(8,128)(2,1)} %param.7), channel_id=1, source_target_pairs={{0,256},{1,304},{2,192},{3,240},{4,128},{5,176},{6,64},{7,112},{8,... | collective-permute-start | bytes 196616 | tf_op jit(solution)/shard_map/ppermute | solution.py:27
  16.9 1.9 %copy-start = (bf16[24,256,256]{2,1,0:T(8,128)(2,1)S(1)}, bf16[24,256,256]{2,1,0:T(8,128)(2,1)}, u32[]{:S(2)}) copy-start(bf16[24,256,256]{2,1,0:T(8,128)(2,1)} %tiles_hbm.1) | copy-start | bytes 9437188
  45.3 11.4 %collective-permute-start.3 = (bf16[8,64,512]{2,1,0:T(8,128)(2,1)S(1)}, bf16[8,64,512]{2,1,0:T(8,128)(2,1)S(1)}, u32[]{:S(2)}, u32[]{:S(2)}) collective-permute-start(bf16[8,64,512]{2,1,0:T(8,128)(2,1)S(1)} %all_to_all.20.b0), channel_id=1, source_target_pairs={{0,16},{1,65},{2,18},{3,67},{4,20},{5,69},{6,22},{7,71},{8,24},{9,... | collective-permute-start | bytes 1572872 | tf_op jit(solution)/shard_map/ppermute | solution.py:27
  47.2 10.2 %collective-permute-start.2 = (bf16[8,64,512]{2,1,0:T(8,128)(2,1)S(1)}, bf16[8,64,512]{2,1,0:T(8,128)(2,1)S(1)}, u32[]{:S(2)}, u32[]{:S(2)}) collective-permute-start(bf16[8,64,512]{2,1,0:T(8,128)(2,1)S(1)} %all_to_all.20.b0), channel_id=1, source_target_pairs={{0,448},{1,49},{2,450},{3,51},{4,452},{5,53},{6,454},{7,55},{8,456... | collective-permute-start | bytes 1572872 | tf_op jit(solution)/shard_map/ppermute | solution.py:27
  49.9 13.3 %collective-permute-start.1 = (bf16[8,64,512]{2,1,0:T(8,128)(2,1)S(1)}, bf16[8,64,512]{2,1,0:T(8,128)(2,1)S(1)}, u32[]{:S(2)}, u32[]{:S(2)}) collective-permute-start(bf16[8,64,512]{2,1,0:T(8,128)(2,1)S(1)} %all_to_all.20.b0), channel_id=1, source_target_pairs={{0,64},{1,17},{2,66},{3,19},{4,68},{5,21},{6,70},{7,23},{8,72},{9,... | collective-permute-start | bytes 1572872 | tf_op jit(solution)/shard_map/ppermute | solution.py:27
  63.2 26.7 %copy-start.1 = (bf16[64,512]{1,0:T(8,128)(2,1)S(1)}, bf16[64,512]{1,0:T(8,128)(2,1)}, u32[]{:S(2)}) copy-start(bf16[64,512]{1,0:T(8,128)(2,1)} %param.7) | copy-start | bytes 196612
  65.0 3.9 %collective-permute-start.4 = (bf16[8,64,512]{2,1,0:T(8,128)(2,1)S(1)}, bf16[8,64,512]{2,1,0:T(8,128)(2,1)S(1)}, u32[]{:S(2)}, u32[]{:S(2)}) collective-permute-start(bf16[8,64,512]{2,1,0:T(8,128)(2,1)S(1)} %get-tuple-element.20), channel_id=1, source_target_pairs={{0,1},{1,0},{2,3},{3,2},{4,5},{5,4},{6,7},{7,6},{8,9},{9,8},{10,11... | collective-permute-start | bytes 1572872 | tf_op jit(solution)/shard_map/ppermute | solution.py:27
  90.0 12.3 %collective-permute-start.5 = (bf16[64,512]{1,0:T(8,128)(2,1)S(1)}, bf16[64,512]{1,0:T(8,128)(2,1)S(1)}, u32[]{:S(2)}, u32[]{:S(2)}) collective-permute-start(bf16[64,512]{1,0:T(8,128)(2,1)S(1)} %fusion.2), channel_id=1, source_target_pairs={{0,256},{1,304},{2,192},{3,240},{4,128},{5,176},{6,64},{7,112},{8,... | collective-permute-start | bytes 196616 | tf_op jit(solution)/shard_map/ppermute | solution.py:27
  120.0 17.3 %collective-permute-start.8 = (bf16[8,64,512]{2,1,0:T(8,128)(2,1)S(1)}, bf16[8,64,512]{2,1,0:T(8,128)(2,1)S(1)}, u32[]{:S(2)}, u32[]{:S(2)}) collective-permute-start(bf16[8,64,512]{2,1,0:T(8,128)(2,1)S(1)} %all_to_all.22.b0), channel_id=1, source_target_pairs={{0,16},{1,65},{2,18},{3,67},{4,20},{5,69},{6,22},{7,71},{8,24},{9,... | collective-permute-start | bytes 1572872 | tf_op jit(solution)/shard_map/ppermute | solution.py:27
  131.2 10.2 %collective-permute-start.7 = (bf16[8,64,512]{2,1,0:T(8,128)(2,1)S(1)}, bf16[8,64,512]{2,1,0:T(8,128)(2,1)S(1)}, u32[]{:S(2)}, u32[]{:S(2)}) collective-permute-start(bf16[8,64,512]{2,1,0:T(8,128)(2,1)S(1)} %all_to_all.22.b0), channel_id=1, source_target_pairs={{0,448},{1,49},{2,450},{3,51},{4,452},{5,53},{6,454},{7,55},{8,456... | collective-permute-start | bytes 1572872 | tf_op jit(solution)/shard_map/ppermute | solution.py:27
  133.1 12.3 %collective-permute-start.6 = (bf16[8,64,512]{2,1,0:T(8,128)(2,1)S(1)}, bf16[8,64,512]{2,1,0:T(8,128)(2,1)S(1)}, u32[]{:S(2)}, u32[]{:S(2)}) collective-permute-start(bf16[8,64,512]{2,1,0:T(8,128)(2,1)S(1)} %all_to_all.22.b0), channel_id=1, source_target_pairs={{0,64},{1,17},{2,66},{3,19},{4,68},{5,21},{6,70},{7,23},{8,72},{9,... | collective-permute-start | bytes 1572872 | tf_op jit(solution)/shard_map/ppermute | solution.py:27
  147.2 3.8 %collective-permute-start.9 = (bf16[8,64,512]{2,1,0:T(8,128)(2,1)S(1)}, bf16[8,64,512]{2,1,0:T(8,128)(2,1)S(1)}, u32[]{:S(2)}, u32[]{:S(2)}) collective-permute-start(bf16[8,64,512]{2,1,0:T(8,128)(2,1)S(1)} %get-tuple-element.24), channel_id=1, source_target_pairs={{0,1},{1,0},{2,3},{3,2},{4,5},{5,4},{6,7},{7,6},{8,9},{9,8},{10,11... | collective-permute-start | bytes 1572872 | tf_op jit(solution)/shard_map/ppermute | solution.py:27

commit v3 on v2

--- a/solution.py
+++ b/solution.py
@@ -100,9 +100,17 @@
     )(tiles)
 
 
-def product_kernel(
-    place_ref, row_ref, core_ref, b0, b1, b2, b3, tiles, keep_ref, give_ref, total
-):
+def product(block, tile):
+    return lax.dot_general(
+        block, tile, (((1,), (1,)), ((), ())), preferred_element_type=jnp.float32
+    )
+
+
+def lane_half(place):
+    return pl.ds(pl.multiple_of((place % 2) * TB, TB), TB)
+
+
+def early_kernel(place_ref, row_ref, own, above, beside, tiles, total):
     total[...] = jnp.zeros_like(total)
     chunk = 6
     for first in range(0, SLOTS, chunk):
@@ -112,21 +120,30 @@
             place = place_ref[slot]
             part = place // 16
             member = (place // 2) % 8
-            columns = pl.ds(pl.multiple_of((place % 2) * TB, TB), TB)
+            columns = lane_half(place)
             block = jnp.where(
-                part < 2,
-                jnp.where(part == 0, b0[member, :, columns], b1[member, :, columns]),
-                jnp.where(part == 2, b2[member, :, columns], b3[member, :, columns]),
+                part == 0,
+                own[member, :, columns],
+                jnp.where(part == 2, above[member, :, columns], beside[member, :, columns]),
             )
-            products.append(
-                lax.dot_general(
-                    block, tiles[slot], (((1,), (1,)), ((), ())),
-                    preferred_element_type=jnp.float32,
-                )
-            )
-        for slot, product in zip(slots, products):
-            row = row_ref[slot]
-            total[row] = total[row] + product
+            products.append(product(block, tiles[slot]))
+        for slot, value in zip(slots, products):
+            row = jnp.where(place_ref[slot] // 16 == 1, BR, row_ref[slot])
+            total[row] = total[row] + value
+
+
+def late_kernel(
+    place_ref, row_ref, core_ref, before, below, tiles, keep_ref, give_ref, total
+):
+    for slot in range(SLOTS):
+        place = place_ref[slot]
+        row = row_ref[slot]
+
+        @pl.when(jnp.logical_and(place // 16 == 1, row < BR))
+        def _():
+            block = below[(place // 2) % 8, :, lane_half(place)]
+            total[row] = total[row] + product(block, tiles[slot])
+
     core = core_ref[0]
     for line in range(NY):
         for half in range(2):
@@ -136,20 +153,30 @@
 
 
 def local_product(parts, tiles, places, rows, core):
+    own, below, above, beside = parts
+    scalars = pl.BlockSpec(memory_space=pltpu.SMEM)
+    whole = pl.BlockSpec(memory_space=pltpu.VMEM)
+    sums = jax.ShapeDtypeStruct((BR + 1, NV, TB), jnp.float32)
     half_panel = jax.ShapeDtypeStruct((NY, NV, PIECE), jnp.bfloat16)
-    return pl.pallas_call(
-        product_kernel,
-        out_shape=(half_panel, half_panel),
-        in_specs=[pl.BlockSpec(memory_space=pltpu.SMEM)] * 3
-        + [pl.BlockSpec(memory_space=pltpu.VMEM)] * 5,
-        out_specs=(pl.BlockSpec(memory_space=pltpu.VMEM),) * 2,
-        scratch_shapes=[pltpu.VMEM((BR + 1, NV, TB), jnp.float32)],
-        compiler_params=pltpu.CompilerParams(vmem_limit_bytes=24 * 1024 * 1024),
-        cost_estimate=pl.CostEstimate(
-            flops=2 * SLOTS * NV * TB * TB, bytes_accessed=8 * 1024 * 1024, transcendentals=0
-        ),
-        name="block_products",
-    )(places, rows, core, *parts, tiles)
+    params = pltpu.CompilerParams(vmem_limit_bytes=24 * 1024 * 1024)
+    total = pl.pallas_call(
+        early_kernel,
+        out_shape=sums,
+        in_specs=[scalars] * 2 + [whole] * 4,
+        out_specs=whole,
+        compiler_params=params,
+        name="early_products",
+    )(places, rows, own, above, beside, tiles)
+    keep, give, _ = pl.pallas_call(
+        late_kernel,
+        out_shape=(half_panel, half_panel, sums),
+        in_specs=[scalars] * 3 + [whole] * 3,
+        out_specs=(whole,) * 3,
+        input_output_aliases={3: 2},
+        compiler_params=params,
+        name="late_products",
+    )(places, rows, core, total, below, tiles)
+    return keep, give
 
 
 def line_sum(keep, taken):

time: 173 us -> 173 us (level)
  starting transfers between devices: 51.1 us -> 46.3 us
  Pallas kernels: 3.89 us -> 8.34 us
  waiting for transfers between devices: 26.3 us -> 24 us
  blocking collectives: 85 us -> 87.2 us
    ppermute x10, starting transfers between devices: 51.1 us -> 46.3 us  [permute(): lax.ppermute(value, AXES, [(number(*p), number(*move(*p))) for p in PLACES])]
    pallas_call x2 -> x4, Pallas kernels: 3.67 us -> 8.12 us  [the longest x2 4.69 us: local_product(): pl.pallas_call(late_kernel, out_shape=(half_panel, half_panel, sums), in_...]
    ppermute x10, waiting for transfers between devices: 26.3 us -> 24 us  [permute(): lax.ppermute(value, AXES, [(number(*p), number(*move(*p))) for p in PLACES])]
    all_to_all x4, blocking collectives: 85 us -> 87.2 us  [exchange(): lax.all_to_all(value, AXES, 0, 0, axis_index_groups=groups, tiled=True)]
  transfers between devices with their start and end apart: 10 -> 10, of which waited for: 9 -> 9; matrix products, arithmetic and copies ran while one was open for 0% -> 0% of each run, Pallas kernels for 0% -> 2%
where the time goes in v3:
time: 173 us; the launch traced here: 172 us
  blocking collectives  87.2 us (50%)
  starting transfers between devices  46.3 us (27%)
  waiting for transfers between devices  24 us (14%)
  Pallas kernels  8.34 us (5%)
  between operations  2.18 us (1%)
  local copies, waits for them, and re-layouts  1.96 us (1%)
  other arithmetic  1.83 us (1%)
    all_to_all x4, blocking collectives, exchange(): lax.all_to_all(value, AXES, 0, 0, axis_index_groups=groups, tiled=True)  87.2 us
    ppermute x10, starting transfers between devices, permute(): lax.ppermute(value, AXES, [(number(*p), number(*move(*p))) for p in PLACES])  46.3 us
    ppermute x10, waiting for transfers between devices, permute(): lax.ppermute(value, AXES, [(number(*p), number(*move(*p))) for p in PLACES])  24 us
    pallas_call x2, Pallas kernels, local_product(): pl.pallas_call(late_kernel, out_shape=(half_panel, half_panel, sums), in_...  4.69 us
  transfers between devices with their start and end apart: 10, of which 9 were waited for; matrix products, arithmetic and copies ran while one was open for 0% of the time, Pallas kernels for 2%

profile of v3, /device:TPU:1, one launch (start us, length us, event | category | flops | bytes accessed | tf_op | source)
XLA Modules:
  0.0 171.8 jit_solution(18021494959295518249)
XLA Ops:
  0.0 14.2 %collective-permute-start = (bf16[64,512]{1,0:T(8,128)(2,1)}, bf16[64,512]{1,0:T(8,128)(2,1)S(1)}, u32[]{:S(2)}, u32[]{:S(2)}) collective-permute-start(bf16[64,512]{1,0:T(8,128)(2,1)} %param.7), channel_id=1, source_target_pairs={{0,256},{1,304},{2,192},{3,240},{4,128},{5,176},{6,64},{7,112},{8,... | collective-permute-start | bytes 196616 | tf_op jit(solution)/shard_map/ppermute | solution.py:27
  14.9 0.7 compare_select_fusion.6
  16.9 0.0 copy-start
  16.9 1.9 %copy-done = bf16[24,256,256]{2,1,0:T(8,128)(2,1)S(1)} copy-done((bf16[24,256,256]{2,1,0:T(8,128)(2,1)S(1)}, bf16[24,256,256]{2,1,0:T(8,128)(2,1)}, u32[]{:S(2)}) %copy-start) | copy-done | bytes 3145752
  18.8 0.2 load_tiles.1.tiles
  19.0 0.0 collective-permute-done
  19.1 26.2 %all_to_all.20.own = bf16[8,64,512]{2,1,0:T(8,128)(2,1)S(1)} all-to-all(bf16[8,64,512]{2,1,0:T(8,128)(2,1)S(1)} %broadcast_in_dim.31), channel_id=1, replica_groups={{0,32,144,176,256,288,400,432},{1,97,129,225,257,353,385,481},{2,34,146..., dimensions={0} | all-to-all | bytes 1048576 | tf_op jit(solution)/shard_map/all_to_all | solution.py:38
  45.3 1.9 %collective-permute-start.2 = (bf16[8,64,512]{2,1,0:T(8,128)(2,1)S(1)}, bf16[8,64,512]{2,1,0:T(8,128)(2,1)S(1)}, u32[]{:S(2)}, u32[]{:S(2)}) collective-permute-start(bf16[8,64,512]{2,1,0:T(8,128)(2,1)S(1)} %all_to_all.20.own), channel_id=1, source_target_pairs={{0,16},{1,65},{2,18},{3,67},{4,20},{5,69},{6,22},{7,71},{8,24},{9,... | collective-permute-start | bytes 1572872 | tf_op jit(solution)/shard_map/ppermute | solution.py:27
  47.2 2.7 %collective-permute-start.1 = (bf16[8,64,512]{2,1,0:T(8,128)(2,1)S(1)}, bf16[8,64,512]{2,1,0:T(8,128)(2,1)S(1)}, u32[]{:S(2)}, u32[]{:S(2)}) collective-permute-start(bf16[8,64,512]{2,1,0:T(8,128)(2,1)S(1)} %all_to_all.20.own), channel_id=1, source_target_pairs={{0,448},{1,49},{2,450},{3,51},{4,452},{5,53},{6,454},{7,55},{8,456... | collective-permute-start | bytes 1572872 | tf_op jit(solution)/shard_map/ppermute | solution.py:27
  49.9 2.6 %collective-permute-start.3 = (bf16[8,64,512]{2,1,0:T(8,128)(2,1)S(1)}, bf16[8,64,512]{2,1,0:T(8,128)(2,1)S(1)}, u32[]{:S(2)}, u32[]{:S(2)}) collective-permute-start(bf16[8,64,512]{2,1,0:T(8,128)(2,1)S(1)} %all_to_all.20.own), channel_id=1, source_target_pairs={{0,64},{1,17},{2,66},{3,19},{4,68},{5,21},{6,70},{7,23},{8,72},{9,... | collective-permute-start | bytes 1572872 | tf_op jit(solution)/shard_map/ppermute | solution.py:27
  52.5 4.2 %collective-permute-done.2.beside = bf16[8,64,512]{2,1,0:T(8,128)(2,1)S(1)} collective-permute-done((bf16[8,64,512]{2,1,0:T(8,128)(2,1)S(1)}, bf16[8,64,512]{2,1,0:T(8,128)(2,1)S(1)}, u32[]{:S(2)}, u32[]{:S(2)}) %collective-permute-start.2) | collective-permute-done | bytes 524320 | tf_op jit(solution)/shard_map/ppermute | solution.py:27
  56.7 0.7 collective-permute-done.1.above
  57.4 1.7 early_products.2.before
  59.1 4.1 %collective-permute-done.3.below = bf16[8,64,512]{2,1,0:T(8,128)(2,1)S(1)} collective-permute-done((bf16[8,64,512]{2,1,0:T(8,128)(2,1)S(1)}, bf16[8,64,512]{2,1,0:T(8,128)(2,1)S(1)}, u32[]{:S(2)}, u32[]{:S(2)}) %collective-permute-start.3) | collective-permute-done | bytes 524320 | tf_op jit(solution)/shard_map/ppermute | solution.py:27
  63.2 2.3 %late_products.2 = (bf16[8,64,512]{2,1,0:T(8,128)(2,1)S(1)}, bf16[8,64,512]{2,1,0:T(8,128)(2,1)S(1)}, f32[33,64,256]{2,1,0:T(8,128)S(1)}) custom-call(s32[24]{0:T(128)S(1)} %get-tuple-element.15.place_ref, s32[24]{0:T(128)S(1)} %get-tuple-element.16.row_ref, s32[1]{0:T(128)} %bitcast.3.core_ref, ...), custom_call_target="tpu_custom_call", output_to_operand_aliasing={{2}: (3, {})} | custom-call | tf_op jit(solution)/shard_map/late_products/pallas_call | solution.py:170
  65.6 0.0 copy-start.1
  65.6 2.1 %collective-permute-start.4 = (bf16[8,64,512]{2,1,0:T(8,128)(2,1)S(1)}, bf16[8,64,512]{2,1,0:T(8,128)(2,1)S(1)}, u32[]{:S(2)}, u32[]{:S(2)}) collective-permute-start(bf16[8,64,512]{2,1,0:T(8,128)(2,1)S(1)} %get-tuple-element.20), channel_id=1, source_target_pairs={{0,1},{1,0},{2,3},{3,2},{4,5},{5,4},{6,7},{7,6},{8,9},{9,8},{10,11... | collective-permute-start | bytes 1572872 | tf_op jit(solution)/shard_map/ppermute | solution.py:27
  67.6 1.9 %collective-permute-done.4 = bf16[8,64,512]{2,1,0:T(8,128)(2,1)S(1)} collective-permute-done((bf16[8,64,512]{2,1,0:T(8,128)(2,1)S(1)}, bf16[8,64,512]{2,1,0:T(8,128)(2,1)S(1)}, u32[]{:S(2)}, u32[]{:S(2)}) %collective-permute-start.4) | collective-permute-done | bytes 524320 | tf_op jit(solution)/shard_map/ppermute | solution.py:27
  69.5 0.1 add_convert_fusion.1
  69.6 21.8 %all_to_all.21 = bf16[8,64,512]{2,1,0:T(8,128)(2,1)S(1)} all-to-all(bf16[8,64,512]{2,1,0:T(8,128)(2,1)S(1)} %add_convert_fusion.1), channel_id=1, replica_groups={{0,2,4,6,8,10,12,14},{1,3,5,7,9,11,13,15},{16,18,20,22,24,26,28,30},{17..., dimensions={0} | all-to-all | bytes 1048576 | tf_op jit(solution)/shard_map/all_to_all | solution.py:38
  91.4 0.1 convert_reduce_fusion.1
  91.5 0.0 copy-done.1
  91.5 7.1 %collective-permute-start.5 = (bf16[64,512]{1,0:T(8,128)(2,1)S(1)}, bf16[64,512]{1,0:T(8,128)(2,1)S(1)}, u32[]{:S(2)}, u32[]{:S(2)}) collective-permute-start(bf16[64,512]{1,0:T(8,128)(2,1)S(1)} %fusion.2), channel_id=1, source_target_pairs={{0,256},{1,304},{2,192},{3,240},{4,128},{5,176},{6,64},{7,112},{8,... | collective-permute-start | bytes 196616 | tf_op jit(solution)/shard_map/ppermute | solution.py:27
  98.7 4.2 %collective-permute-done.5 = bf16[64,512]{1,0:T(8,128)(2,1)S(1)} collective-permute-done((bf16[64,512]{1,0:T(8,128)(2,1)S(1)}, bf16[64,512]{1,0:T(8,128)(2,1)S(1)}, u32[]{:S(2)}, u32[]{:S(2)}) %collective-permute-start.5) | collective-permute-done | bytes 65568 | tf_op jit(solution)/shard_map/ppermute | solution.py:27
  102.9 18.8 %all_to_all.22.own = bf16[8,64,512]{2,1,0:T(8,128)(2,1)S(1)} all-to-all(bf16[8,64,512]{2,1,0:T(8,128)(2,1)S(1)} %broadcast_in_dim.32), channel_id=1, replica_groups={{0,32,144,176,256,288,400,432},{1,97,129,225,257,353,385,481},{2,34,146..., dimensions={0} | all-to-all | bytes 1048576 | tf_op jit(solution)/shard_map/all_to_all | solution.py:38
  121.7 8.4 %collective-permute-start.7 = (bf16[8,64,512]{2,1,0:T(8,128)(2,1)S(1)}, bf16[8,64,512]{2,1,0:T(8,128)(2,1)S(1)}, u32[]{:S(2)}, u32[]{:S(2)}) collective-permute-start(bf16[8,64,512]{2,1,0:T(8,128)(2,1)S(1)} %all_to_all.22.own), channel_id=1, source_target_pairs={{0,16},{1,65},{2,18},{3,67},{4,20},{5,69},{6,22},{7,71},{8,24},{9,... | collective-permute-start | bytes 1572872 | tf_op jit(solution)/shard_map/ppermute | solution.py:27
  130.1 1.9 %collective-permute-start.6 = (bf16[8,64,512]{2,1,0:T(8,128)(2,1)S(1)}, bf16[8,64,512]{2,1,0:T(8,128)(2,1)S(1)}, u32[]{:S(2)}, u32[]{:S(2)}) collective-permute-start(bf16[8,64,512]{2,1,0:T(8,128)(2,1)S(1)} %all_to_all.22.own), channel_id=1, source_target_pairs={{0,448},{1,49},{2,450},{3,51},{4,452},{5,53},{6,454},{7,55},{8,456... | collective-permute-start | bytes 1572872 | tf_op jit(solution)/shard_map/ppermute | solution.py:27
  132.0 3.4 %collective-permute-start.8 = (bf16[8,64,512]{2,1,0:T(8,128)(2,1)S(1)}, bf16[8,64,512]{2,1,0:T(8,128)(2,1)S(1)}, u32[]{:S(2)}, u32[]{:S(2)}) collective-permute-start(bf16[8,64,512]{2,1,0:T(8,128)(2,1)S(1)} %all_to_all.22.own), channel_id=1, source_target_pairs={{0,64},{1,17},{2,66},{3,19},{4,68},{5,21},{6,70},{7,23},{8,72},{9,... | collective-permute-start | bytes 1572872 | tf_op jit(solution)/shard_map/ppermute | solution.py:27
  135.4 1.0 collective-permute-done.7.beside
  136.4 3.9 %collective-permute-done.6.above = bf16[8,64,512]{2,1,0:T(8,128)(2,1)S(1)} collective-permute-done((bf16[8,64,512]{2,1,0:T(8,128)(2,1)S(1)}, bf16[8,64,512]{2,1,0:T(8,128)(2,1)S(1)}, u32[]{:S(2)}, u32[]{:S(2)}) %collective-permute-start.6) | collective-permute-done | bytes 524320 | tf_op jit(solution)/shard_map/ppermute | solution.py:27
  140.3 1.7 early_products.3.before
  142.0 2.3 %collective-permute-done.8.below = bf16[8,64,512]{2,1,0:T(8,128)(2,1)S(1)} collective-permute-done((bf16[8,64,512]{2,1,0:T(8,128)(2,1)S(1)}, bf16[8,64,512]{2,1,0:T(8,128)(2,1)S(1)}, u32[]{:S(2)}, u32[]{:S(2)}) %collective-permute-start.8) | collective-permute-done | bytes 524320 | tf_op jit(solution)/shard_map/ppermute | solution.py:27
  144.3 2.3 %late_products.3 = (bf16[8,64,512]{2,1,0:T(8,128)(2,1)S(1)}, bf16[8,64,512]{2,1,0:T(8,128)(2,1)S(1)}, f32[33,64,256]{2,1,0:T(8,128)S(1)}) custom-call(s32[24]{0:T(128)S(1)} %get-tuple-element.15.place_ref, s32[24]{0:T(128)S(1)} %get-tuple-element.16.row_ref, s32[1]{0:T(128)} %bitcast.3.core_ref, ...), custom_call_target="tpu_custom_call", output_to_operand_aliasing={{2}: (3, {})} | custom-call | tf_op jit(solution)/shard_map/late_products/pallas_call | solution.py:170
  146.7 2.1 %collective-permute-start.9 = (bf16[8,64,512]{2,1,0:T(8,128)(2,1)S(1)}, bf16[8,64,512]{2,1,0:T(8,128)(2,1)S(1)}, u32[]{:S(2)}, u32[]{:S(2)}) collective-permute-start(bf16[8,64,512]{2,1,0:T(8,128)(2,1)S(1)} %get-tuple-element.24), channel_id=1, source_target_pairs={{0,1},{1,0},{2,3},{3,2},{4,5},{5,4},{6,7},{7,6},{8,9},{9,8},{10,11... | collective-permute-start | bytes 1572872 | tf_op jit(solution)/shard_map/ppermute | solution.py:27
  148.8 1.7 collective-permute-done.9
  150.5 0.1 add_convert_fusion
  150.7 20.4 %all_to_all.23 = bf16[8,64,512]{2,1,0:T(8,128)(2,1)S(1)} all-to-all(bf16[8,64,512]{2,1,0:T(8,128)(2,1)S(1)} %add_convert_fusion), channel_id=1, replica_groups={{0,2,4,6,8,10,12,14},{1,3,5,7,9,11,13,15},{16,18,20,22,24,26,28,30},{17..., dimensions={0} | all-to-all | bytes 1048576 | tf_op jit(solution)/shard_map/all_to_all | solution.py:38
  171.0 0.1 convert_reduce_fusion
  171.1 0.7 fusion.3
  (3 shorter events, 0.1 us)
Async XLA Ops:
  0.0 19.0 %collective-permute-start = (bf16[64,512]{1,0:T(8,128)(2,1)}, bf16[64,512]{1,0:T(8,128)(2,1)S(1)}, u32[]{:S(2)}, u32[]{:S(2)}) collective-permute-start(bf16[64,512]{1,0:T(8,128)(2,1)} %param.7), channel_id=1, source_target_pairs={{0,256},{1,304},{2,192},{3,240},{4,128},{5,176},{6,64},{7,112},{8,... | collective-permute-start | bytes 196616 | tf_op jit(solution)/shard_map/ppermute | solution.py:27
  16.9 1.9 %copy-start = (bf16[24,256,256]{2,1,0:T(8,128)(2,1)S(1)}, bf16[24,256,256]{2,1,0:T(8,128)(2,1)}, u32[]{:S(2)}) copy-start(bf16[24,256,256]{2,1,0:T(8,128)(2,1)} %tiles_hbm.1) | copy-start | bytes 9437188
  45.3 11.4 %collective-permute-start.2 = (bf16[8,64,512]{2,1,0:T(8,128)(2,1)S(1)}, bf16[8,64,512]{2,1,0:T(8,128)(2,1)S(1)}, u32[]{:S(2)}, u32[]{:S(2)}) collective-permute-start(bf16[8,64,512]{2,1,0:T(8,128)(2,1)S(1)} %all_to_all.20.own), channel_id=1, source_target_pairs={{0,16},{1,65},{2,18},{3,67},{4,20},{5,69},{6,22},{7,71},{8,24},{9,... | collective-permute-start | bytes 1572872 | tf_op jit(solution)/shard_map/ppermute | solution.py:27
  47.2 10.2 %collective-permute-start.1 = (bf16[8,64,512]{2,1,0:T(8,128)(2,1)S(1)}, bf16[8,64,512]{2,1,0:T(8,128)(2,1)S(1)}, u32[]{:S(2)}, u32[]{:S(2)}) collective-permute-start(bf16[8,64,512]{2,1,0:T(8,128)(2,1)S(1)} %all_to_all.20.own), channel_id=1, source_target_pairs={{0,448},{1,49},{2,450},{3,51},{4,452},{5,53},{6,454},{7,55},{8,456... | collective-permute-start | bytes 1572872 | tf_op jit(solution)/shard_map/ppermute | solution.py:27
  49.9 13.3 %collective-permute-start.3 = (bf16[8,64,512]{2,1,0:T(8,128)(2,1)S(1)}, bf16[8,64,512]{2,1,0:T(8,128)(2,1)S(1)}, u32[]{:S(2)}, u32[]{:S(2)}) collective-permute-start(bf16[8,64,512]{2,1,0:T(8,128)(2,1)S(1)} %all_to_all.20.own), channel_id=1, source_target_pairs={{0,64},{1,17},{2,66},{3,19},{4,68},{5,21},{6,70},{7,23},{8,72},{9,... | collective-permute-start | bytes 1572872 | tf_op jit(solution)/shard_map/ppermute | solution.py:27
  65.6 26.0 %copy-start.1 = (bf16[64,512]{1,0:T(8,128)(2,1)S(1)}, bf16[64,512]{1,0:T(8,128)(2,1)}, u32[]{:S(2)}) copy-start(bf16[64,512]{1,0:T(8,128)(2,1)} %param.7) | copy-start | bytes 196612
  65.6 3.9 %collective-permute-start.4 = (bf16[8,64,512]{2,1,0:T(8,128)(2,1)S(1)}, bf16[8,64,512]{2,1,0:T(8,128)(2,1)S(1)}, u32[]{:S(2)}, u32[]{:S(2)}) collective-permute-start(bf16[8,64,512]{2,1,0:T(8,128)(2,1)S(1)} %get-tuple-element.20), channel_id=1, source_target_pairs={{0,1},{1,0},{2,3},{3,2},{4,5},{5,4},{6,7},{7,6},{8,9},{9,8},{10,11... | collective-permute-start | bytes 1572872 | tf_op jit(solution)/shard_map/ppermute | solution.py:27
  91.5 11.3 %collective-permute-start.5 = (bf16[64,512]{1,0:T(8,128)(2,1)S(1)}, bf16[64,512]{1,0:T(8,128)(2,1)S(1)}, u32[]{:S(2)}, u32[]{:S(2)}) collective-permute-start(bf16[64,512]{1,0:T(8,128)(2,1)S(1)} %fusion.2), channel_id=1, source_target_pairs={{0,256},{1,304},{2,192},{3,240},{4,128},{5,176},{6,64},{7,112},{8,... | collective-permute-start | bytes 196616 | tf_op jit(solution)/shard_map/ppermute | solution.py:27
  121.7 14.7 %collective-permute-start.7 = (bf16[8,64,512]{2,1,0:T(8,128)(2,1)S(1)}, bf16[8,64,512]{2,1,0:T(8,128)(2,1)S(1)}, u32[]{:S(2)}, u32[]{:S(2)}) collective-permute-start(bf16[8,64,512]{2,1,0:T(8,128)(2,1)S(1)} %all_to_all.22.own), channel_id=1, source_target_pairs={{0,16},{1,65},{2,18},{3,67},{4,20},{5,69},{6,22},{7,71},{8,24},{9,... | collective-permute-start | bytes 1572872 | tf_op jit(solution)/shard_map/ppermute | solution.py:27
  130.1 10.2 %collective-permute-start.6 = (bf16[8,64,512]{2,1,0:T(8,128)(2,1)S(1)}, bf16[8,64,512]{2,1,0:T(8,128)(2,1)S(1)}, u32[]{:S(2)}, u32[]{:S(2)}) collective-permute-start(bf16[8,64,512]{2,1,0:T(8,128)(2,1)S(1)} %all_to_all.22.own), channel_id=1, source_target_pairs={{0,448},{1,49},{2,450},{3,51},{4,452},{5,53},{6,454},{7,55},{8,456... | collective-permute-start | bytes 1572872 | tf_op jit(solution)/shard_map/ppermute | solution.py:27
  132.0 12.4 %collective-permute-start.8 = (bf16[8,64,512]{2,1,0:T(8,128)(2,1)S(1)}, bf16[8,64,512]{2,1,0:T(8,128)(2,1)S(1)}, u32[]{:S(2)}, u32[]{:S(2)}) collective-permute-start(bf16[8,64,512]{2,1,0:T(8,128)(2,1)S(1)} %all_to_all.22.own), channel_id=1, source_target_pairs={{0,64},{1,17},{2,66},{3,19},{4,68},{5,21},{6,70},{7,23},{8,72},{9,... | collective-permute-start | bytes 1572872 | tf_op jit(solution)/shard_map/ppermute | solution.py:27
  146.7 3.8 %collective-permute-start.9 = (bf16[8,64,512]{2,1,0:T(8,128)(2,1)S(1)}, bf16[8,64,512]{2,1,0:T(8,128)(2,1)S(1)}, u32[]{:S(2)}, u32[]{:S(2)}) collective-permute-start(bf16[8,64,512]{2,1,0:T(8,128)(2,1)S(1)} %get-tuple-element.24), channel_id=1, source_target_pairs={{0,1},{1,0},{2,3},{3,2},{4,5},{5,4},{6,7},{7,6},{8,9},{9,8},{10,11... | collective-permute-start | bytes 1572872 | tf_op jit(solution)/shard_map/ppermute | solution.py:27
